TPU v7x, 128 devices: a whole 4x4x4 slice. The times are simulated.
128 devices in a mesh: lon: 16 (over x, y_hi, core), lat: 8 (over z, y_lo).
Axes of the slice: x: 4, y: 4 (y_hi: 2, y_lo: 2; y = y_hi * 2 + y_lo), z: 4, core: 2. Of those that a mesh axis runs over, the one named last changes fastest.
Arguments:
- features: bfloat16 [32768, 4096], P(('lon', 'lat')), may hold values from 0.0099487305 to 1
- cosine_zenith: bfloat16 [32768], P(('lon', 'lat')), may hold values from 0.049804688 to 1
- albedo: bfloat16 [2, 32768], P(None, ('lon', 'lat')), may hold values from 0.049804688 to 0.84765625
- sunlit: int32 [32768], P(('lon', 'lat')), may hold values 0 or 1
- column_map: int32 [32768], P(('lon', 'lat')), may hold values from -1 to 16383, as said below
- swap_list: int32 [8192], P(('lon', 'lat')), may hold values from 0 to 127, as said below
- gas_table: bfloat16 [64, 224], replicated, may hold values from 0 to 5
- asymmetry: float32 [112], replicated, may hold values from 0 to 0.8
- solar_source: float32 [112], replicated, may hold values from 0.5 to 2
Outputs:
- absorbed: float32 [64, 32768], P(None, ('lon', 'lat'))
- group_mean: float32 [128, 64], P(('lon', 'lat'))
Inputs may be any that keep to these rules, and one draw needn't show every extreme that they name: `column_map`: A value t names place t of the groups (group t // 128, slot t % 128); -1 marks an empty owner slot. Every place is named exactly once. The slots of one owner device name at most 4 places of one group, and in every draw some owner names exactly 4 places of some group; in every draw some owner device has all 256 slots live. `swap_list`: entries k * 64 to (k + 1) * 64 - 1 are 64 distinct slots of group k.
All inputs are finite; a program needn't handle non-finite values. No bound on the sum of `sunlit` on one device may be relied on, other than what follows from the above.
Results may differ from a plain program's by a relative error of at most 0.0003.
Values may be sent and summed in bfloat16 or wider, within the bound.
A program may use at most 128 MiB of HBM per device.

v0:
```python
import functools
import jax
import jax.numpy as jnp
from jax import lax
from jax.sharding import PartitionSpec as P
from jax.experimental import pallas as pl
from jax.experimental.pallas import tpu as pltpu

LEV = 64
NF = 64
G = 112
LANES = 128
SUB = 8
GB = G // SUB
PAIRS = LEV // 2
LOG2E = 1.4426950408889634


def recip(x):
    return pl.reciprocal(x, approx=True)


def column_kernel(
    feat_ref, cosine_ref, albedo_ref, sunlit_ref, map_ref, gas_ref, asym_ref, solar_ref,
    out_ref,
    weight_ref, depth_ref, const_ref, state_ref, gain_ref, add_ref, admit_ref, down_ref, net_ref,
):
    f32 = jnp.float32
    bf16 = jnp.bfloat16

    table = gas_ref[...]
    stacked = jnp.concatenate([table, table], axis=0)
    row = lax.broadcasted_iota(jnp.int32, (2 * G, 2 * G), 0)
    col = lax.broadcasted_iota(jnp.int32, (2 * G, 2 * G), 1)
    unit = jnp.where(row == col, 1.0, 0.0).astype(bf16)
    turned = lax.dot_general(unit, stacked, (((1,), (1,)), ((), ())), preferred_element_type=f32)
    tau_rows = 2.0 * (turned[:G] + turned[G:])
    ray_rows = (2.0 * 0.98) * turned[G:]
    lane = lax.broadcasted_iota(jnp.int32, (G, LANES), 1)
    for part, value in enumerate((tau_rows, ray_rows)):
        high = value.astype(bf16).astype(f32)
        low = value - high
        for parity in range(2):
            keep = (lane < NF) if parity == 0 else (lane >= NF)
            at = (2 * parity + part) * G
            weight_ref[at : at + G, :LANES] = jnp.where(keep, high, 0.0).astype(bf16)
            weight_ref[at : at + G, LANES:] = jnp.where(keep, low, 0.0).astype(bf16)

    def to_rows(line):
        wide = jnp.broadcast_to(line, (LANES, G))
        return wide.T

    asym = to_rows(asym_ref[...])
    solar = to_rows(solar_ref[...])
    const_ref[0] = 0.25 * (1.0 + 3.0 * asym)
    const_ref[1] = 0.5 - 0.25 * asym

    cosine = cosine_ref[...].astype(f32)
    day = sunlit_ref[...].astype(f32)
    slant = jnp.broadcast_to(-0.5 * LOG2E / cosine, (SUB, LANES))
    state_ref[0] = solar * (cosine * day)
    state_ref[1] = jnp.ones((G, LANES), f32)
    state_ref[2] = jnp.zeros((G, LANES), f32)
    state_ref[3] = jnp.zeros((G, LANES), f32)

    def optical(pair, slot):
        chunk = feat_ref[:, pl.ds(pl.multiple_of(pair * LANES, LANES), LANES)]
        twice = jnp.concatenate([chunk, chunk], axis=1)
        depth_ref[slot] = lax.dot_general(
            weight_ref[...], twice, (((1,), (1,)), ((), ())), preferred_element_type=f32
        )

    optical(0, 0)

    def down(pair, carry):
        slot = lax.rem(pair, 2)
        optical(jnp.minimum(pair + 1, PAIRS - 1), 1 - slot)
        totals = [jnp.zeros((SUB, LANES), f32) for _ in range(2)]
        for g in range(GB):
            rows = pl.ds(g * SUB, SUB)
            direct, admit, source, left = (state_ref[n, rows, :] for n in range(4))
            slope = const_ref[0, rows, :]
            back = const_ref[1, rows, :]
            for odd in range(2):
                layer = 2 * pair + odd
                tau = depth_ref[slot, pl.ds(2 * odd * G + g * SUB, SUB), :]
                ray = depth_ref[slot, pl.ds((2 * odd + 1) * G + g * SUB, SUB), :]
                single = ray * recip(tau)
                f_one = 1.0 - single
                f_two = 1.0 - single * slope
                root = lax.rsqrt(f_one * f_two)
                sigma = f_one * root
                x = f_two * sigma * tau
                th = jnp.tanh(x)
                e = jnp.exp2(x * (-LOG2E))
                sech = e + e * th
                trans = jnp.exp2(tau * slant)
                below = direct * trans
                scattered = single * (direct - below)
                up = back * scattered
                dn = scattered - up
                jump = up - left
                totals[odd] = totals[odd] + (source + direct)
                inner = source + up - admit * jump
                z = recip(sigma + admit * th)
                zs = z * sigma
                gain = sech * zs
                gain_ref[layer, rows, :] = gain
                add_ref[layer, rows, :] = (th * z) * inner + jump
                admit_ref[layer, rows, :] = admit
                admit = (admit + sigma * th) * zs
                source = gain * inner + dn
                direct = below
                left = dn
            for n, value in enumerate((direct, admit, source, left)):
                state_ref[n, rows, :] = value
        for odd in range(2):
            down_ref[2 * pair + odd] = totals[odd]
        return carry

    lax.fori_loop(0, PAIRS, down, 0)

    alb_dir = jnp.broadcast_to(albedo_ref[0:1, :].astype(f32), (SUB, LANES))
    alb_dif = jnp.broadcast_to(albedo_ref[1:2, :].astype(f32), (SUB, LANES))
    fluxes = []
    total = jnp.zeros((SUB, LANES), f32)
    for g in range(GB):
        rows = pl.ds(g * SUB, SUB)
        direct, admit, source, left = (state_ref[n, rows, :] for n in range(4))
        over = source * (1.0 + alb_dif) + 2.0 * alb_dir * direct - left * (1.0 - alb_dif)
        flux = over / ((1.0 - alb_dif) + admit * (1.0 + alb_dif))
        total = total + (direct + source - admit * flux)
        fluxes.append(flux)
    net_ref[LEV : LEV + 1, :] = jnp.sum(total, axis=0, keepdims=True)

    def upward(step, carry):
        layer = LEV - 1 - step
        total = down_ref[layer]
        out = []
        for g in range(GB):
            rows = pl.ds(g * SUB, SUB)
            flux = gain_ref[layer, rows, :] * carry[g] + add_ref[layer, rows, :]
            total = total - admit_ref[layer, rows, :] * flux
            out.append(flux)
        net_ref[pl.ds(layer, 1), :] = jnp.sum(total, axis=0, keepdims=True)
        return tuple(out)

    lax.fori_loop(0, LEV, upward, tuple(fluxes))
    live = map_ref[...] >= 0
    absorbed = net_ref[0:LEV, :] - net_ref[1 : LEV + 1, :]
    out_ref[...] = jnp.where(live, absorbed, 0.0)


def columns_absorbed(features, cosine, albedo, sunlit, column_map, gas_table, asymmetry, solar):
    count = features.shape[0]
    blocks = count // LANES
    line = lambda n: pl.BlockSpec((n, LANES), lambda i: (0, i))
    whole = lambda shape: pl.BlockSpec(shape, lambda i: (0,) * len(shape))
    return pl.pallas_call(
        column_kernel,
        grid=(blocks,),
        out_shape=jax.ShapeDtypeStruct((LEV, count), jnp.float32),
        in_specs=[
            pl.BlockSpec((LANES, LEV * NF), lambda i: (i, 0)),
            line(1), line(2), line(1), line(1),
            whole((NF, 2 * G)), whole((1, G)), whole((1, G)),
        ],
        out_specs=pl.BlockSpec((LEV, LANES), lambda i: (0, i)),
        scratch_shapes=[
            pltpu.VMEM((4 * G, 2 * LANES), jnp.bfloat16),
            pltpu.VMEM((2, 4 * G, LANES), jnp.float32),
            pltpu.VMEM((2, G, LANES), jnp.float32),
            pltpu.VMEM((4, G, LANES), jnp.float32),
            pltpu.VMEM((LEV, G, LANES), jnp.float32),
            pltpu.VMEM((LEV, G, LANES), jnp.float32),
            pltpu.VMEM((LEV, G, LANES), jnp.float32),
            pltpu.VMEM((LEV, SUB, LANES), jnp.float32),
            pltpu.VMEM((LEV + SUB, LANES), jnp.float32),
        ],
        compiler_params=pltpu.CompilerParams(vmem_limit_bytes=32 * 1024 * 1024),
        cost_estimate=pl.CostEstimate(flops=200_000_000, bytes_accessed=2_200_000, transcendentals=10_000_000),
    )(features, cosine[None], albedo, sunlit[None], column_map[None], gas_table, asymmetry[None], solar[None])


def group_means(absorbed, column_map, swap_list):
    axes = ("lon", "lat")
    groups = lax.axis_size("lon") * lax.axis_size("lat")
    slots = jnp.arange(LANES, dtype=jnp.int32)
    lists = lax.all_gather(swap_list, axes, axis=0, tiled=False)
    swapped = jnp.any(lists[:, :, None] == slots[None, None, :], axis=1)
    home = column_map // LANES
    place = column_map % LANES
    moved = swapped[jnp.maximum(home, 0), place]
    held = jnp.where(moved, (home + groups // 2) % groups, home)
    held = jnp.where(column_map >= 0, held, -1)
    member = (held[None, :] == jnp.arange(groups, dtype=jnp.int32)[:, None]).astype(jnp.float32)
    sums = lax.dot_general(
        member, absorbed, (((1,), (1,)), ((), ())), precision=lax.Precision.HIGHEST
    )
    mine = lax.psum_scatter(sums, axes, scatter_dimension=0, tiled=True)
    return mine * (1.0 / LANES)


def body(
    features, cosine_zenith, albedo, sunlit, column_map, swap_list, gas_table, asymmetry, solar_source
):
    absorbed = columns_absorbed(
        features, cosine_zenith, albedo, sunlit, column_map, gas_table, asymmetry, solar_source
    )
    return absorbed, group_means(absorbed, column_map, swap_list)


def solution(mesh):
    both = ("lon", "lat")
    in_specs = (
        P(both, None), P(both), P(None, both), P(both), P(both), P(both), P(), P(), P(),
    )
    out_specs = (P(None, both), P(both, None))
    return jax.shard_map(body, mesh=mesh, in_specs=in_specs, out_specs=out_specs, check_vma=False)
```

profile of v0, /device:TPU:1, one launch (start us, length us, event | category | flops | bytes accessed | tf_op | source)
XLA Modules:
  0.0 176.5 jit_solution(14741824812613361269)
XLA Ops:
  0.6 0.7 broadcast_in_dim.27.cosine_ref
  1.3 0.7 shift-left_or_fusion
  2.0 0.9 dynamic-update-slice
  2.9 68.8 %all-reduce = s32[8192]{0:T(1024)S(1)} all-reduce(s32[8192]{0:T(1024)S(1)} %dynamic-update-slice), channel_id=2, replica_groups=mesh['lon'=16,'lat'=8] {'lon','lat'}, use_global_device_ids=true, to_apply=%add | all-reduce | flops 8192 | bytes 65536
  71.7 0.1 reshape.12
  71.8 1.4 fusion
  73.2 2.4 %gather_fusion = pred[256]{0:T(512)(128)(4,1)S(1)} fusion(pred[128,128]{1,0:T(8,128)(4,1)S(1)} %fusion, s32[256]{0:T(256)S(1)} %get-tuple-element.2), kind=kCustom, calls=%fused_computation | custom fusion | bytes 2560 | tf_op jit(solution)/shard_map/gather | solution.py:193
  75.6 0.7 compare_select_fusion.3
  76.3 0.0 copy-start
  76.3 0.7 copy-done
  77.0 0.0 copy-start.1
  77.0 1.6 copy-done.1
  78.6 0.0 copy-start.2
  78.6 0.8 copy-done.2
  79.3 0.0 copy-start.3
  79.3 0.7 copy-done.3
  80.0 0.0 copy-start.4
  80.0 0.7 copy-done.4
  80.7 0.0 copy-start.5
  80.7 0.7 copy-done.5
  81.3 0.0 copy-start.6
  81.3 0.7 copy-done.6
  82.0 30.2 %shard_map.104 = f32[64,256]{1,0:T(8,128)} custom-call(bf16[256,4096]{1,0:T(8,128)(2,1)S(1)} %copy-done.1, bf16[1,256]{1,0:T(2,128)(2,1)S(1)} %broadcast_in_dim.27.cosine_ref, bf16[2,256]{1,0:T(2,128)(2,1)S(1)} %copy-done.3, s32[1,256]{1,0:T(1,128)S(1)} %bitcast.6, s32[1,256]{1,0:T(1,128)S(1)} %bitcast.5, bf16[64,224]{1,0:T(8,128)(2,1)S(1)} %copy-done.2, ...), custom_call_target="tpu_custom_call" | custom-call | flops 200000000 | bytes 2200000 | tf_op jit(solution)/shard_map/pallas_call | solution.py:159
  112.2 1.0 fusion.1
  113.3 62.7 %all-reduce.1 = f32[128,64]{1,0:T(8,128)S(1)} all-reduce(f32[128,64]{1,0:T(8,128)S(1)} %fusion.1), channel_id=3, replica_groups=mesh['lon'=16,'lat'=8] {'lon','lat'}, use_global_device_ids=true, to_apply=%region_1.2.clone | all-reduce | flops 8192 | bytes 65536
  176.0 0.5 dynamic-slice_multiply_fusion
  (1 shorter events, 0.0 us)
Async XLA Ops:
  76.3 0.7 copy-start
  77.0 1.6 copy-start.1
  78.6 0.8 copy-start.2
  79.3 0.7 copy-start.3
  80.0 0.7 copy-start.4
  80.7 0.7 copy-start.5
  81.3 0.7 copy-start.6
where the time goes:
time: 177 us; the launch traced here: 176 us
  blocking collectives  132 us (75%)
  Pallas kernels  30.2 us (17%)
  local copies, waits for them, and re-layouts  9.7 us (5%)
  other arithmetic  3.3 us (2%)
    unnamed x2, blocking collectives  132 us
    pallas_call x1, Pallas kernels, columns_absorbed(): pl.pallas_call(column_kernel, grid=(blocks,), out_shape=jax.ShapeDtypeStr...  30.2 us
    unnamed x16, local copies, waits for them, and re-layouts  6.56 us

commit v1 on v0

v1 whole, which is shorter than its diff:
```python
import functools
import jax
import jax.numpy as jnp
from jax import lax
from jax.sharding import PartitionSpec as P
from jax.experimental import pallas as pl
from jax.experimental.pallas import tpu as pltpu

LEV = 64
NF = 64
G = 112
HALF_G = G // 2
LANES = 128
SUB = 8
GB = HALF_G // SUB
PAIRS = LEV // 2
SLOTS = 256
BLOCK = 64
KINDS = 5
LOG2E = 1.4426950408889634
NT = (((1,), (1,)), ((), ()))
NN = (((1,), (0,)), ((), ()))


def recip(x):
    return pl.reciprocal(x, approx=True)


def mxu(a, b, dims):
    return lax.dot_general(a, b, dims, preferred_element_type=jnp.float32)


def column_kernel(
    feat_hbm, cosine_hbm, albedo_hbm, sunlit_hbm, map_hbm, gas_hbm, asym_hbm, solar_hbm,
    out_ref,
    feat_ref, cosine_ref, albedo_ref, sunlit_ref, map_ref, gas_ref, asym_ref, solar_ref,
    packed_ref, weight_ref, spread_ref, surface_ref, solar_rows_ref, depth_a, depth_b, depth_c, depth_d,
    state_ref, gain_ref, add_ref, admit_ref, down_ref, net_ref, small_sem, feat_sem,
):
    f32 = jnp.float32
    bf16 = jnp.bfloat16
    chunks = [
        pltpu.make_async_copy(
            feat_hbm.at[:, pl.ds(n * 1024, 1024)], feat_ref.at[:, pl.ds(n * 1024, 1024)], feat_sem.at[n]
        )
        for n in range(4)
    ]
    small = [
        pltpu.make_async_copy(src, dst, small_sem.at[n])
        for n, (src, dst) in enumerate(
            (
                (sunlit_hbm, sunlit_ref), (map_hbm, map_ref), (cosine_hbm, cosine_ref),
                (albedo_hbm, albedo_ref), (gas_hbm, gas_ref), (asym_hbm, asym_ref), (solar_hbm, solar_ref),
            )
        )
    ]
    for copy in small:
        copy.start()
    for copy in chunks:
        copy.start()
    for copy in small:
        copy.wait()

    day = sunlit_ref[...].astype(f32)
    lit = jnp.where((map_ref[...] >= 0) & (sunlit_ref[...] != 0), 1.0, 0.0)
    count = jnp.sum(lit).astype(jnp.int32)
    row = lax.broadcasted_iota(jnp.int32, (SLOTS, SLOTS), 0)
    col = lax.broadcasted_iota(jnp.int32, (SLOTS, SLOTS), 1)
    upper = jnp.where(row <= col, 1.0, 0.0).astype(bf16)
    rank = mxu(jnp.broadcast_to(lit, (SUB, SLOTS)).astype(bf16), upper, NN)[0:1]
    rank = jnp.where(lit > 0.0, rank, 0.0).astype(jnp.int32) - 1
    pick = jnp.where(rank == row, 1.0, 0.0).astype(bf16)
    for n in range(SLOTS // BLOCK):
        part = pick[n * BLOCK : (n + 1) * BLOCK]
        spread_ref[n, :BLOCK, :] = part
        spread_ref[n, BLOCK:, :] = part
    faces = jnp.concatenate(
        [cosine_ref[...].astype(f32), albedo_ref[...].astype(f32), day, jnp.zeros((4, SLOTS), f32)], axis=0
    ).astype(bf16)
    for n in range(SLOTS // BLOCK):
        surface_ref[n] = mxu(faces, spread_ref[n], NT)

    table = gas_ref[...]
    stacked = jnp.concatenate([table, table], axis=0)
    unit = jnp.where(row == col, 1.0, 0.0)[: 2 * G, : 2 * G].astype(bf16)
    turned = mxu(unit, stacked, NT)
    first = lax.broadcasted_iota(jnp.int32, (HALF_G, LANES), 1) < BLOCK

    def halves(rows, at):
        return jnp.where(first, rows[at : at + HALF_G], rows[at + HALF_G : at + G])

    def to_rows(line):
        return halves(jnp.broadcast_to(line, (LANES, G)).T, 0)

    asym = to_rows(asym_ref[...])
    solar_rows_ref[...] = to_rows(solar_ref[...])
    absorb = halves(turned, 0)
    scatter = halves(turned, G)
    quantities = (
        absorb + scatter,
        2.0 * absorb + (2.0 - 2.0 * 0.98) * scatter,
        2.0 * absorb + (2.0 - 0.49 * (1.0 + 3.0 * asym)) * scatter,
        0.98 * (0.5 - 0.25 * asym) * scatter,
        0.98 * (0.5 + 0.25 * asym) * scatter,
    )
    for n, value in enumerate(quantities):
        high = value.astype(bf16)
        weight_ref[n * HALF_G : (n + 1) * HALF_G, :LANES] = high
        weight_ref[n * HALF_G : (n + 1) * HALF_G, LANES:] = (value - high.astype(f32)).astype(bf16)

    for n in range(4):
        chunks[n].wait()

        def pack(step, carry):
            at = pl.ds(pl.multiple_of(n * 1024 + step * 256, 256), 256)
            packed_ref[:, at] = mxu(pick, feat_ref[:, at], NN).astype(bf16)
            return carry

        lax.fori_loop(0, 4, pack, 0)

    out_ref[...] = jnp.zeros((LEV, SLOTS), f32)
    low_lanes = lax.broadcasted_iota(jnp.int32, (BLOCK, LANES), 1) < BLOCK
    nothing = jnp.zeros((BLOCK, LANES), bf16)

    def one_block(block, carry):
        faces_here = surface_ref[block]
        lane = lax.broadcasted_iota(jnp.int32, (1, LANES), 1)
        within = jnp.where(lane >= BLOCK, lane - BLOCK, lane) + block * BLOCK < count
        cosine = jnp.where(within, faces_here[0:1], 1.0)
        slant = jnp.broadcast_to(-LOG2E / cosine, (SUB, LANES))
        alb_dir = jnp.broadcast_to(faces_here[1:2], (SUB, LANES))
        alb_dif = jnp.broadcast_to(faces_here[2:3], (SUB, LANES))
        state_ref[0] = solar_rows_ref[...] * (cosine * faces_here[3:4])
        state_ref[1] = jnp.ones((HALF_G, LANES), f32)
        state_ref[2] = jnp.zeros((HALF_G, LANES), f32)
        state_ref[3] = jnp.zeros((HALF_G, LANES), f32)

        def optical(pair, depth):
            chunk = packed_ref[
                pl.ds(pl.multiple_of(block * BLOCK, BLOCK), BLOCK),
                pl.ds(pl.multiple_of(pair * LANES, LANES), LANES),
            ]
            turn = jnp.concatenate([chunk[:, BLOCK:], chunk[:, :BLOCK]], axis=1)
            both = jnp.concatenate(
                [
                    jnp.where(low_lanes, chunk, nothing),
                    jnp.where(low_lanes, nothing, turn),
                    jnp.where(low_lanes, turn, nothing),
                    jnp.where(low_lanes, nothing, chunk),
                ],
                axis=0,
            )
            depth[...] = mxu(weight_ref[...], jnp.concatenate([both, both], axis=1), NT)

        def one_pair(pair, depth):
            totals = [jnp.zeros((SUB, LANES), f32) for _ in range(2)]
            for g in range(GB):
                rows = pl.ds(g * SUB, SUB)
                direct, admit, source, left = (state_ref[n, rows, :] for n in range(4))
                for odd in range(2):
                    layer = 2 * pair + odd
                    tau, t_one, t_two, to_up, to_dn = (
                        depth[n * HALF_G + g * SUB : n * HALF_G + (g + 1) * SUB, odd * LANES : (odd + 1) * LANES]
                        for n in range(KINDS)
                    )
                    product = t_one * t_two
                    root = lax.rsqrt(product)
                    x = product * root
                    sigma = t_one * root
                    th = jnp.tanh(x)
                    e = jnp.exp2(x * (-LOG2E))
                    sech = e + e * th
                    below = direct * jnp.exp2(tau * slant)
                    lost = (direct - below) * recip(tau)
                    up = to_up * lost
                    dn = to_dn * lost
                    jump = up - left
                    totals[odd] = totals[odd] + (source + direct)
                    inner = source + up - admit * jump
                    z = recip(sigma + admit * th)
                    zs = z * sigma
                    gain = sech * zs
                    gain_ref[layer, rows, :] = gain
                    add_ref[layer, rows, :] = (th * z) * inner + jump
                    admit_ref[layer, rows, :] = admit
                    admit = (admit + sigma * th) * zs
                    source = gain * inner + dn
                    direct = below
                    left = dn
                for n, value in enumerate((direct, admit, source, left)):
                    state_ref[n, rows, :] = value
            for odd in range(2):
                down_ref[2 * pair + odd] = totals[odd]

        optical(0, depth_a)
        optical(1, depth_b)

        def down(step, inner_carry):
            @pl.when(count > 0)
            def _():
                one_pair(4 * step, depth_a)
                one_pair(4 * step + 1, depth_b)
                optical(4 * step + 2, depth_c)
                optical(4 * step + 3, depth_d)

            @pl.when(count > 0)
            def _():
                one_pair(4 * step + 2, depth_c)
                one_pair(4 * step + 3, depth_d)
                optical(jnp.minimum(4 * step + 4, PAIRS - 2), depth_a)
                optical(jnp.minimum(4 * step + 5, PAIRS - 1), depth_b)

            return inner_carry

        lax.fori_loop(0, PAIRS // 4, down, 0)

        fluxes = []
        total = jnp.zeros((SUB, LANES), f32)
        for g in range(GB):
            rows = pl.ds(g * SUB, SUB)
            direct, admit, source, left = (state_ref[n, rows, :] for n in range(4))
            over = source * (1.0 + alb_dif) + 2.0 * alb_dir * direct - left * (1.0 - alb_dif)
            flux = over / ((1.0 - alb_dif) + admit * (1.0 + alb_dif))
            total = total + (direct + source - admit * flux)
            fluxes.append(flux)
        net_ref[LEV : LEV + 1, :] = jnp.sum(total, axis=0, keepdims=True)

        def upward(step, fluxes):
            for odd in range(4):
                layer = LEV - 1 - 4 * step - odd
                total = down_ref[layer]
                out = []
                for g in range(GB):
                    rows = pl.ds(g * SUB, SUB)
                    flux = gain_ref[layer, rows, :] * fluxes[g] + add_ref[layer, rows, :]
                    total = total - admit_ref[layer, rows, :] * flux
                    out.append(flux)
                fluxes = tuple(out)
                net_ref[pl.ds(layer, 1), :] = jnp.sum(total, axis=0, keepdims=True)
            return fluxes

        lax.fori_loop(0, LEV // 4, upward, tuple(fluxes))
        absorbed = jnp.where(within, net_ref[0:LEV, :] - net_ref[1 : LEV + 1, :], 0.0)
        high = absorbed.astype(bf16)
        low = (absorbed - high.astype(f32)).astype(bf16)
        home = spread_ref[block]
        out_ref[...] += mxu(high, home, NN) + mxu(low, home, NN)
        return carry

    lax.fori_loop(0, lax.div(count + (BLOCK - 1), BLOCK), one_block, 0)


def columns_absorbed(features, cosine, albedo, sunlit, column_map, gas_table, asymmetry, solar):
    anywhere = pl.BlockSpec(memory_space=pl.ANY)
    f32, bf16, i32 = jnp.float32, jnp.bfloat16, jnp.int32
    return pl.pallas_call(
        column_kernel,
        out_shape=jax.ShapeDtypeStruct((LEV, SLOTS), f32),
        in_specs=[anywhere] * 8,
        out_specs=pl.BlockSpec(memory_space=pltpu.VMEM),
        scratch_shapes=[
            pltpu.VMEM((SLOTS, LEV * NF), bf16),
            pltpu.VMEM((1, SLOTS), bf16),
            pltpu.VMEM((2, SLOTS), bf16),
            pltpu.VMEM((1, SLOTS), i32),
            pltpu.VMEM((1, SLOTS), i32),
            pltpu.VMEM((NF, 2 * G), bf16),
            pltpu.VMEM((1, G), f32),
            pltpu.VMEM((1, G), f32),
            pltpu.VMEM((SLOTS, LEV * NF), bf16),
            pltpu.VMEM((KINDS * HALF_G, 2 * LANES), bf16),
            pltpu.VMEM((SLOTS // BLOCK, LANES, SLOTS), bf16),
            pltpu.VMEM((SLOTS // BLOCK, SUB, LANES), f32),
            pltpu.VMEM((HALF_G, LANES), f32),
            pltpu.VMEM((KINDS * HALF_G, 2 * LANES), f32),
            pltpu.VMEM((KINDS * HALF_G, 2 * LANES), f32),
            pltpu.VMEM((KINDS * HALF_G, 2 * LANES), f32),
            pltpu.VMEM((KINDS * HALF_G, 2 * LANES), f32),
            pltpu.VMEM((4, HALF_G, LANES), f32),
            pltpu.VMEM((LEV, HALF_G, LANES), f32),
            pltpu.VMEM((LEV, HALF_G, LANES), f32),
            pltpu.VMEM((LEV, HALF_G, LANES), f32),
            pltpu.VMEM((LEV, SUB, LANES), f32),
            pltpu.VMEM((LEV + SUB, LANES), f32),
            pltpu.SemaphoreType.DMA((7,)),
            pltpu.SemaphoreType.DMA((4,)),
        ],
        compiler_params=pltpu.CompilerParams(vmem_limit_bytes=60 * 1024 * 1024),
        cost_estimate=pl.CostEstimate(flops=200_000_000, bytes_accessed=2_200_000, transcendentals=10_000_000),
    )(features, cosine[None], albedo, sunlit[None], column_map[None], gas_table, asymmetry[None], solar[None])


def mean_kernel(absorbed_ref, map_ref, swap_ref, mean_ref, own_ref, row_ref, mask_ref, part_ref, first_ref, strip_ref, second_ref, send_a, recv_a, send_b, recv_b, send_c, recv_c, send_d, recv_d):
    f32 = jnp.float32
    bf16 = jnp.bfloat16
    n_lon, n_lat = lax.axis_size("lon"), lax.axis_size("lat")
    lon, lat = lax.axis_index("lon"), lax.axis_index("lat")
    groups = n_lon * n_lat
    lon_peers = [lax.rem(lon + d, n_lon) for d in range(n_lon)]
    lat_peers = [lax.rem(lat + d, n_lat) for d in range(n_lat)]

    barrier = pltpu.get_barrier_semaphore()
    for d in range(1, n_lat):
        pl.semaphore_signal(barrier, inc=1, device_id=(lon, lat_peers[d]), device_id_type=pl.DeviceIdType.MESH)
    for d in range(1, n_lon):
        pl.semaphore_signal(barrier, inc=1, device_id=(lon_peers[d], lat), device_id_type=pl.DeviceIdType.MESH)

    listed = jnp.broadcast_to(swap_ref[...].astype(f32), (LANES, LANES // 2)).T
    lane = lax.broadcasted_iota(jnp.int32, (LANES // 2, LANES), 1).astype(f32)
    mine = jnp.max(jnp.where(listed == lane, 1.0, 0.0), axis=0, keepdims=True)
    own_ref[0] = mine
    row_ref[lat] = mine
    pl.semaphore_wait(barrier, n_lat + n_lon - 2)

    def send(src, dst, sends, recvs, d, device):
        copy = pltpu.make_async_remote_copy(
            src_ref=src, dst_ref=dst, send_sem=sends.at[d], recv_sem=recvs.at[d],
            device_id=device, device_id_type=pl.DeviceIdType.MESH,
        )
        copy.start()
        return copy

    along_lat = lambda d: (lon, lat_peers[d])
    along_lon = lambda d: (lon_peers[d], lat)
    copies = [send(own_ref.at[0], row_ref.at[lat], send_a, recv_a, d, along_lat(d)) for d in range(1, n_lat)]
    for copy in copies:
        copy.wait()
    mask_ref[lon] = row_ref[...]
    copies = [send(row_ref, mask_ref.at[lon], send_b, recv_b, d, along_lon(d)) for d in range(1, n_lon)]

    place = map_ref[...]
    home = lax.shift_right_arithmetic(place, 7)
    slot = place & (LANES - 1)
    row = lax.broadcasted_iota(jnp.int32, (groups, SLOTS), 0)
    at_home = jnp.where(home == row, 1.0, 0.0).astype(bf16)
    at_slot = jnp.where(slot == lax.broadcasted_iota(jnp.int32, (LANES, SLOTS), 0), 1.0, 0.0)
    absorbed = absorbed_ref[...]
    absorbed = jnp.concatenate([absorbed, jnp.zeros((LANES - LEV, SLOTS), f32)], axis=0)
    high = absorbed.astype(bf16)
    low = (absorbed - high.astype(f32)).astype(bf16)
    for copy in copies:
        copy.wait()

    masks = mask_ref[...].reshape(groups, LANES)
    listed_at = mxu(masks.T.astype(bf16), at_home, NN)
    moved = jnp.sum(listed_at * at_slot, axis=0, keepdims=True)
    away = jnp.where(home >= groups // 2, home - groups // 2, home + groups // 2)
    held = jnp.where(place < 0, -1, jnp.where(moved > 0.5, away, home))
    member = jnp.where(held == row, 1.0, 0.0).astype(bf16)
    sums = mxu(member, high, NT) + mxu(member, low, NT)
    part_ref[...] = sums.reshape(n_lon, n_lat, LANES)

    copies = [send(part_ref.at[lon_peers[d]], first_ref.at[d], send_c, recv_c, d, along_lon(d)) for d in range(1, n_lon)]
    total = part_ref[lon]
    for d, copy in enumerate(copies):
        copy.wait()
    for d in range(1, n_lon):
        total = total + first_ref[d]
    for n in range(n_lat):
        strip_ref[n] = total[n : n + 1]

    copies = [send(strip_ref.at[lat_peers[d]], second_ref.at[d], send_d, recv_d, d, along_lat(d)) for d in range(1, n_lat)]
    total = strip_ref[lat]
    for copy in copies:
        copy.wait()
    for d in range(1, n_lat):
        total = total + second_ref[d]
    mean_ref[...] = total[:, :LEV] * (1.0 / LANES)


def group_means(absorbed, column_map, swap_list):
    n_lon, n_lat = lax.axis_size("lon"), lax.axis_size("lat")
    f32 = jnp.float32
    vmem = pl.BlockSpec(memory_space=pltpu.VMEM)
    dma = pltpu.SemaphoreType.DMA
    return pl.pallas_call(
        mean_kernel,
        out_shape=jax.ShapeDtypeStruct((1, LEV), f32),
        in_specs=[vmem] * 3,
        out_specs=vmem,
        scratch_shapes=[
            pltpu.VMEM((1, 1, LANES), f32),
            pltpu.VMEM((n_lat, 1, LANES), f32),
            pltpu.VMEM((n_lon, n_lat, 1, LANES), f32),
            pltpu.VMEM((n_lon, n_lat, LANES), f32),
            pltpu.VMEM((n_lon, n_lat, LANES), f32),
            pltpu.VMEM((n_lat, 1, LANES), f32),
            pltpu.VMEM((n_lat, 1, LANES), f32),
            dma((n_lat,)), dma((n_lat,)), dma((n_lon,)), dma((n_lon,)),
            dma((n_lon,)), dma((n_lon,)), dma((n_lat,)), dma((n_lat,)),
        ],
        compiler_params=pltpu.CompilerParams(collective_id=0, has_side_effects=True, vmem_limit_bytes=60 * 1024 * 1024),
        cost_estimate=pl.CostEstimate(flops=20_000_000, bytes_accessed=200_000, transcendentals=0),
    )(absorbed, column_map[None], swap_list[None])


def body(
    features, cosine_zenith, albedo, sunlit, column_map, swap_list, gas_table, asymmetry, solar_source
):
    absorbed = columns_absorbed(
        features, cosine_zenith, albedo, sunlit, column_map, gas_table, asymmetry, solar_source
    )
    return absorbed, group_means(absorbed, column_map, swap_list)


def solution(mesh):
    both = ("lon", "lat")
    in_specs = (
        P(both, None), P(both), P(None, both), P(both), P(both), P(both), P(), P(), P(),
    )
    out_specs = (P(None, both), P(both, None))
    return jax.shard_map(body, mesh=mesh, in_specs=in_specs, out_specs=out_specs, check_vma=False)
```

time: 177 us -> 52 us (0.29)
  blocking collectives: 132 us -> 0 us
  Pallas kernels: 30.2 us -> 48.8 us
  local copies, waits for them, and re-layouts: 9.7 us -> 2.44 us
  other arithmetic: 3.3 us -> 0 us
    unnamed x2 -> x0, blocking collectives: 132 us -> none
    pallas_call x1 -> x2, Pallas kernels: 30.2 us -> 48.8 us  [the longest x1 37.6 us: group_means(): pl.pallas_call(mean_kernel, out_shape=jax.ShapeDtypeStruct((1, LEV), f32)...]
    unnamed x16 -> x1, local copies, waits for them, and re-layouts: 6.56 us -> 1.19 us
    gather x1 -> x0, local copies, waits for them, and re-layouts: 2.41 us -> none  [group_means(): moved = swapped[jnp.maximum(home, 0), place]]
where the time goes in v1:
time: 52 us; the launch traced here: 51.8 us
  Pallas kernels  48.8 us (94%)
  local copies, waits for them, and re-layouts  2.44 us (5%)
  between operations  0.65 us (1%)
    pallas_call x1, Pallas kernels, group_means(): pl.pallas_call(mean_kernel, out_shape=jax.ShapeDtypeStruct((1, LEV), f32)...  37.6 us
    pallas_call x1, Pallas kernels, columns_absorbed(): pl.pallas_call(column_kernel, out_shape=jax.ShapeDtypeStruct((LEV, SLOTS)...  11.1 us
    broadcast_in_dim x1, local copies, waits for them, and re-layouts, columns_absorbed(): cosine[None]  1.25 us
    unnamed x1, local copies, waits for them, and re-layouts  1.19 us

profile of v1, /device:TPU:1, one launch (start us, length us, event | category | flops | bytes accessed | tf_op | source)
XLA Modules:
  0.0 51.8 jit_solution(14510982713323036299)
XLA Ops:
  0.6 1.2 %broadcast_in_dim.19.cosine_hbm = bf16[1,256]{1,0:T(2,128)(2,1)} reshape(bf16[256]{0:T(256)(128)(2,1)} %param.10) | data formatting | bytes 1024 | tf_op jit(solution)/shard_map/broadcast_in_dim | solution.py:290
  1.9 11.1 %shard_map.104.absorbed_ref = f32[64,256]{1,0:T(8,128)} custom-call(bf16[256,4096]{1,0:T(8,128)(2,1)} %feat_hbm.1, bf16[1,256]{1,0:T(2,128)(2,1)} %broadcast_in_dim.19.cosine_hbm, bf16[2,256]{1,0:T(2,128)(2,1)} %albedo_hbm.1, s32[1,256]{1,0:T(1,128)} %bitcast.5, s32[1,256]{1,0:T(1,128)} %bitcast.6, bf16[64,224]{1,0:T(8,128)(2,1)} %gas_hbm.1, ...), custom_call_target="tpu_custom_call" | custom-call | flops 200000000 | bytes 2200000 | tf_op jit(solution)/shard_map/pallas_call | solution.py:256
  13.0 37.6 %shard_map.105 = f32[1,64]{1,0:T(1,128)} custom-call(f32[64,256]{1,0:T(8,128)} %shard_map.104.absorbed_ref, s32[1,256]{1,0:T(1,128)} %bitcast.7, s32[1,64]{1,0:T(1,128)} %bitcast.10), custom_call_target="tpu_custom_call" | custom-call | flops 20000000 | bytes 200000 | tf_op jit(solution)/shard_map/pallas_call | solution.py:376
  50.7 1.2 %copy.12 = f32[1,64]{1,0:T(1,128)} copy(f32[1,64]{1,0:T(1,128)} %shard_map.105) | data formatting | bytes 512

commit v2 on v1

--- a/solution.py
+++ b/solution.py
@@ -31,11 +31,12 @@
 
 
 def column_kernel(
-    feat_hbm, cosine_hbm, albedo_hbm, sunlit_hbm, map_hbm, gas_hbm, asym_hbm, solar_hbm,
-    out_ref,
-    feat_ref, cosine_ref, albedo_ref, sunlit_ref, map_ref, gas_ref, asym_ref, solar_ref,
+    feat_hbm, cosine_hbm, albedo_hbm, sunlit_hbm, map_hbm, gas_hbm, asym_hbm, solar_hbm, swap_hbm,
+    out_ref, mean_ref,
+    feat_ref, cosine_ref, albedo_ref, sunlit_ref, map_ref, gas_ref, asym_ref, solar_ref, swap_ref,
     packed_ref, weight_ref, spread_ref, surface_ref, solar_rows_ref, depth_a, depth_b, depth_c, depth_d,
-    state_ref, gain_ref, add_ref, admit_ref, down_ref, net_ref, small_sem, feat_sem,
+    state_ref, gain_ref, add_ref, admit_ref, down_ref, net_ref, own_ref, mask_ref, part_ref, other_ref, strip_ref, last_ref,
+    small_sem, feat_sem, send_a, recv_a, send_b, recv_b, send_c, recv_c,
 ):
     f32 = jnp.float32
     bf16 = jnp.bfloat16
@@ -51,6 +52,7 @@
             (
                 (sunlit_hbm, sunlit_ref), (map_hbm, map_ref), (cosine_hbm, cosine_ref),
                 (albedo_hbm, albedo_ref), (gas_hbm, gas_ref), (asym_hbm, asym_ref), (solar_hbm, solar_ref),
+                (swap_hbm, swap_ref),
             )
         )
     ]
@@ -58,8 +60,37 @@
         copy.start()
     for copy in chunks:
         copy.start()
+
+    n_lon, n_lat = lax.axis_size("lon"), lax.axis_size("lat")
+    lon, lat = lax.axis_index("lon"), lax.axis_index("lat")
+    groups = n_lon * n_lat
+    chips = groups // 2
+    core = lax.rem(lon, 2)
+    chip = lax.div(lon, 2) * n_lat + lat
+    mesh_ids = pl.DeviceIdType.MESH
+    sibling = (lon + 1 - 2 * core, lat)
+    peers = [
+        (lax.rem(lon + 2 * a, n_lon), lax.rem(lat + c, n_lat))
+        for a in range(n_lon // 2) for c in range(n_lat) if a or c
+    ]
+    barrier = pltpu.get_barrier_semaphore()
+    for device in [sibling] + peers:
+        pl.semaphore_signal(barrier, inc=1, device_id=device, device_id_type=mesh_ids)
+
+    def remote(src, dst, sends, recvs, n, device):
+        copy = pltpu.make_async_remote_copy(
+            src_ref=src, dst_ref=dst, send_sem=sends.at[n], recv_sem=recvs.at[n],
+            device_id=device, device_id_type=mesh_ids,
+        )
+        copy.start()
+        return copy
+
     for copy in small:
         copy.wait()
+
+    listed = jnp.broadcast_to(swap_ref[...].astype(f32), (LANES, LANES // 2)).T
+    lane_no = lax.broadcasted_iota(jnp.int32, (LANES // 2, LANES), 1).astype(f32)
+    own_ref[0] = jnp.max(jnp.where(listed == lane_no, 1.0, 0.0), axis=0, keepdims=True)
 
     day = sunlit_ref[...].astype(f32)
     lit = jnp.where((map_ref[...] >= 0) & (sunlit_ref[...] != 0), 1.0, 0.0)
@@ -196,20 +227,14 @@
         optical(1, depth_b)
 
         def down(step, inner_carry):
-            @pl.when(count > 0)
-            def _():
-                one_pair(4 * step, depth_a)
-                one_pair(4 * step + 1, depth_b)
-                optical(4 * step + 2, depth_c)
-                optical(4 * step + 3, depth_d)
-
-            @pl.when(count > 0)
-            def _():
-                one_pair(4 * step + 2, depth_c)
-                one_pair(4 * step + 3, depth_d)
-                optical(jnp.minimum(4 * step + 4, PAIRS - 2), depth_a)
-                optical(jnp.minimum(4 * step + 5, PAIRS - 1), depth_b)
-
+            one_pair(4 * step, depth_a)
+            one_pair(4 * step + 1, depth_b)
+            optical(4 * step + 2, depth_c)
+            optical(4 * step + 3, depth_d)
+            one_pair(4 * step + 2, depth_c)
+            one_pair(4 * step + 3, depth_d)
+            optical(jnp.minimum(4 * step + 4, PAIRS - 2), depth_a)
+            optical(jnp.minimum(4 * step + 5, PAIRS - 1), depth_b)
             return inner_carry
 
         lax.fori_loop(0, PAIRS // 4, down, 0)
@@ -247,17 +272,66 @@
         out_ref[...] += mxu(high, home, NN) + mxu(low, home, NN)
         return carry
 
-    lax.fori_loop(0, lax.div(count + (BLOCK - 1), BLOCK), one_block, 0)
-
-
-def columns_absorbed(features, cosine, albedo, sunlit, column_map, gas_table, asymmetry, solar):
+    lax.fori_loop(0, 1, one_block, 0)
+
+    pl.semaphore_wait(barrier, chips)
+    mask_ref[core, chip] = own_ref[0]
+    copies = [
+        remote(own_ref.at[0], mask_ref.at[core, chip], send_a, recv_a, n, device)
+        for n, device in enumerate(peers)
+    ]
+    lax.fori_loop(1, 2, one_block, 0)
+    for copy in copies:
+        copy.wait()
+    copy = remote(mask_ref.at[core], mask_ref.at[core], send_b, recv_b, 0, sibling)
+    lax.fori_loop(2, 4, one_block, 0)
+    copy.wait()
+
+    place = map_ref[...]
+    home = lax.shift_right_arithmetic(place, 7)
+    home_core = lax.rem(lax.div(home, n_lat), 2)
+    home_chip = lax.div(home, 2 * n_lat) * n_lat + lax.rem(home, n_lat)
+    away_chip = jnp.where(home_chip >= chips // 2, home_chip - chips // 2, home_chip + chips // 2)
+    slot = place & (LANES - 1)
+    group_row = lax.broadcasted_iota(jnp.int32, (groups, SLOTS), 0)
+    at_home = jnp.where(home_core * chips + home_chip == group_row, 1.0, 0.0).astype(bf16)
+    at_slot = jnp.where(slot == lax.broadcasted_iota(jnp.int32, (LANES, SLOTS), 0), 1.0, 0.0)
+    masks = mask_ref[...].reshape(groups, LANES)
+    listed_at = mxu(masks.T.astype(bf16), at_home, NN)
+    moved = jnp.sum(listed_at * at_slot, axis=0, keepdims=True)
+    held = home_core * chips + jnp.where(moved > 0.5, away_chip, home_chip)
+    held = jnp.where(place < 0, -1, held)
+    member = jnp.where(held == group_row, 1.0, 0.0).astype(bf16)
+    absorbed = jnp.concatenate([out_ref[...], jnp.zeros((LANES - LEV, SLOTS), f32)], axis=0)
+    high = absorbed.astype(bf16)
+    low = (absorbed - high.astype(f32)).astype(bf16)
+    part_ref[...] = (mxu(member, high, NT) + mxu(member, low, NT)).reshape(2, chips, LANES)
+
+    copy = remote(part_ref.at[1 - core], other_ref, send_b, recv_b, 1, sibling)
+    copy.wait()
+    strip_ref[...] = (part_ref[core] + other_ref[...]).reshape(chips, 1, LANES)
+    copies = [
+        remote(strip_ref.at[lax.div(device[0], 2) * n_lat + device[1]], last_ref.at[n], send_c, recv_c, n, device)
+        for n, device in enumerate(peers)
+    ]
+    for copy in copies:
+        copy.wait()
+    total = strip_ref[chip] + jnp.sum(last_ref[...], axis=0)
+    mean_ref[...] = total[:, :LEV] * (1.0 / LANES)
+
+
+def columns_absorbed(features, cosine, albedo, sunlit, column_map, swap_list, gas_table, asymmetry, solar):
     anywhere = pl.BlockSpec(memory_space=pl.ANY)
+    vmem = pl.BlockSpec(memory_space=pltpu.VMEM)
     f32, bf16, i32 = jnp.float32, jnp.bfloat16, jnp.int32
+    n_lon, n_lat = lax.axis_size("lon"), lax.axis_size("lat")
+    chips = n_lon * n_lat // 2
+    dma = pltpu.SemaphoreType.DMA
     return pl.pallas_call(
         column_kernel,
-        out_shape=jax.ShapeDtypeStruct((LEV, SLOTS), f32),
-        in_specs=[anywhere] * 8,
-        out_specs=pl.BlockSpec(memory_space=pltpu.VMEM),
+        out_shape=(jax.ShapeDtypeStruct((LEV, SLOTS), f32), jax.ShapeDtypeStruct((1, LEV), f32)),
+        in_specs=[anywhere] * 9,
+        out_specs=(vmem, vmem),
         scratch_shapes=[
             pltpu.VMEM((SLOTS, LEV * NF), bf16),
             pltpu.VMEM((1, SLOTS), bf16),
@@ -267,6 +341,7 @@
             pltpu.VMEM((NF, 2 * G), bf16),
             pltpu.VMEM((1, G), f32),
             pltpu.VMEM((1, G), f32),
+            pltpu.VMEM((1, LANES // 2), i32),
             pltpu.VMEM((SLOTS, LEV * NF), bf16),
             pltpu.VMEM((KINDS * HALF_G, 2 * LANES), bf16),
             pltpu.VMEM((SLOTS // BLOCK, LANES, SLOTS), bf16),
@@ -282,125 +357,25 @@
             pltpu.VMEM((LEV, HALF_G, LANES), f32),
             pltpu.VMEM((LEV, SUB, LANES), f32),
             pltpu.VMEM((LEV + SUB, LANES), f32),
-            pltpu.SemaphoreType.DMA((7,)),
-            pltpu.SemaphoreType.DMA((4,)),
-        ],
-        compiler_params=pltpu.CompilerParams(vmem_limit_bytes=60 * 1024 * 1024),
-        cost_estimate=pl.CostEstimate(flops=200_000_000, bytes_accessed=2_200_000, transcendentals=10_000_000),
-    )(features, cosine[None], albedo, sunlit[None], column_map[None], gas_table, asymmetry[None], solar[None])
-
-
-def mean_kernel(absorbed_ref, map_ref, swap_ref, mean_ref, own_ref, row_ref, mask_ref, part_ref, first_ref, strip_ref, second_ref, send_a, recv_a, send_b, recv_b, send_c, recv_c, send_d, recv_d):
-    f32 = jnp.float32
-    bf16 = jnp.bfloat16
-    n_lon, n_lat = lax.axis_size("lon"), lax.axis_size("lat")
-    lon, lat = lax.axis_index("lon"), lax.axis_index("lat")
-    groups = n_lon * n_lat
-    lon_peers = [lax.rem(lon + d, n_lon) for d in range(n_lon)]
-    lat_peers = [lax.rem(lat + d, n_lat) for d in range(n_lat)]
-
-    barrier = pltpu.get_barrier_semaphore()
-    for d in range(1, n_lat):
-        pl.semaphore_signal(barrier, inc=1, device_id=(lon, lat_peers[d]), device_id_type=pl.DeviceIdType.MESH)
-    for d in range(1, n_lon):
-        pl.semaphore_signal(barrier, inc=1, device_id=(lon_peers[d], lat), device_id_type=pl.DeviceIdType.MESH)
-
-    listed = jnp.broadcast_to(swap_ref[...].astype(f32), (LANES, LANES // 2)).T
-    lane = lax.broadcasted_iota(jnp.int32, (LANES // 2, LANES), 1).astype(f32)
-    mine = jnp.max(jnp.where(listed == lane, 1.0, 0.0), axis=0, keepdims=True)
-    own_ref[0] = mine
-    row_ref[lat] = mine
-    pl.semaphore_wait(barrier, n_lat + n_lon - 2)
-
-    def send(src, dst, sends, recvs, d, device):
-        copy = pltpu.make_async_remote_copy(
-            src_ref=src, dst_ref=dst, send_sem=sends.at[d], recv_sem=recvs.at[d],
-            device_id=device, device_id_type=pl.DeviceIdType.MESH,
-        )
-        copy.start()
-        return copy
-
-    along_lat = lambda d: (lon, lat_peers[d])
-    along_lon = lambda d: (lon_peers[d], lat)
-    copies = [send(own_ref.at[0], row_ref.at[lat], send_a, recv_a, d, along_lat(d)) for d in range(1, n_lat)]
-    for copy in copies:
-        copy.wait()
-    mask_ref[lon] = row_ref[...]
-    copies = [send(row_ref, mask_ref.at[lon], send_b, recv_b, d, along_lon(d)) for d in range(1, n_lon)]
-
-    place = map_ref[...]
-    home = lax.shift_right_arithmetic(place, 7)
-    slot = place & (LANES - 1)
-    row = lax.broadcasted_iota(jnp.int32, (groups, SLOTS), 0)
-    at_home = jnp.where(home == row, 1.0, 0.0).astype(bf16)
-    at_slot = jnp.where(slot == lax.broadcasted_iota(jnp.int32, (LANES, SLOTS), 0), 1.0, 0.0)
-    absorbed = absorbed_ref[...]
-    absorbed = jnp.concatenate([absorbed, jnp.zeros((LANES - LEV, SLOTS), f32)], axis=0)
-    high = absorbed.astype(bf16)
-    low = (absorbed - high.astype(f32)).astype(bf16)
-    for copy in copies:
-        copy.wait()
-
-    masks = mask_ref[...].reshape(groups, LANES)
-    listed_at = mxu(masks.T.astype(bf16), at_home, NN)
-    moved = jnp.sum(listed_at * at_slot, axis=0, keepdims=True)
-    away = jnp.where(home >= groups // 2, home - groups // 2, home + groups // 2)
-    held = jnp.where(place < 0, -1, jnp.where(moved > 0.5, away, home))
-    member = jnp.where(held == row, 1.0, 0.0).astype(bf16)
-    sums = mxu(member, high, NT) + mxu(member, low, NT)
-    part_ref[...] = sums.reshape(n_lon, n_lat, LANES)
-
-    copies = [send(part_ref.at[lon_peers[d]], first_ref.at[d], send_c, recv_c, d, along_lon(d)) for d in range(1, n_lon)]
-    total = part_ref[lon]
-    for d, copy in enumerate(copies):
-        copy.wait()
-    for d in range(1, n_lon):
-        total = total + first_ref[d]
-    for n in range(n_lat):
-        strip_ref[n] = total[n : n + 1]
-
-    copies = [send(strip_ref.at[lat_peers[d]], second_ref.at[d], send_d, recv_d, d, along_lat(d)) for d in range(1, n_lat)]
-    total = strip_ref[lat]
-    for copy in copies:
-        copy.wait()
-    for d in range(1, n_lat):
-        total = total + second_ref[d]
-    mean_ref[...] = total[:, :LEV] * (1.0 / LANES)
-
-
-def group_means(absorbed, column_map, swap_list):
-    n_lon, n_lat = lax.axis_size("lon"), lax.axis_size("lat")
-    f32 = jnp.float32
-    vmem = pl.BlockSpec(memory_space=pltpu.VMEM)
-    dma = pltpu.SemaphoreType.DMA
-    return pl.pallas_call(
-        mean_kernel,
-        out_shape=jax.ShapeDtypeStruct((1, LEV), f32),
-        in_specs=[vmem] * 3,
-        out_specs=vmem,
-        scratch_shapes=[
             pltpu.VMEM((1, 1, LANES), f32),
-            pltpu.VMEM((n_lat, 1, LANES), f32),
-            pltpu.VMEM((n_lon, n_lat, 1, LANES), f32),
-            pltpu.VMEM((n_lon, n_lat, LANES), f32),
-            pltpu.VMEM((n_lon, n_lat, LANES), f32),
-            pltpu.VMEM((n_lat, 1, LANES), f32),
-            pltpu.VMEM((n_lat, 1, LANES), f32),
-            dma((n_lat,)), dma((n_lat,)), dma((n_lon,)), dma((n_lon,)),
-            dma((n_lon,)), dma((n_lon,)), dma((n_lat,)), dma((n_lat,)),
+            pltpu.VMEM((2, chips, 1, LANES), f32),
+            pltpu.VMEM((2, chips, LANES), f32),
+            pltpu.VMEM((chips, LANES), f32),
+            pltpu.VMEM((chips, 1, LANES), f32),
+            pltpu.VMEM((chips - 1, 1, LANES), f32),
+            dma((8,)), dma((4,)), dma((chips,)), dma((chips,)), dma((2,)), dma((2,)), dma((chips,)), dma((chips,)),
         ],
         compiler_params=pltpu.CompilerParams(collective_id=0, has_side_effects=True, vmem_limit_bytes=60 * 1024 * 1024),
-        cost_estimate=pl.CostEstimate(flops=20_000_000, bytes_accessed=200_000, transcendentals=0),
-    )(absorbed, column_map[None], swap_list[None])
+        cost_estimate=pl.CostEstimate(flops=200_000_000, bytes_accessed=2_200_000, transcendentals=10_000_000),
+    )(features, cosine[None], albedo, sunlit[None], column_map[None], gas_table, asymmetry[None], solar[None], swap_list[None])
 
 
 def body(
     features, cosine_zenith, albedo, sunlit, column_map, swap_list, gas_table, asymmetry, solar_source
 ):
-    absorbed = columns_absorbed(
-        features, cosine_zenith, albedo, sunlit, column_map, gas_table, asymmetry, solar_source
+    return columns_absorbed(
+        features, cosine_zenith, albedo, sunlit, column_map, swap_list, gas_table, asymmetry, solar_source
     )
-    return absorbed, group_means(absorbed, column_map, swap_list)
 
 
 def solution(mesh):

time: 52 us -> 47.8 us (0.919)
  Pallas kernels: 48.8 us -> 43.2 us
  local copies, waits for them, and re-layouts: 2.44 us -> 3.81 us
    pallas_call x2 -> x1, Pallas kernels: 48.8 us -> 43.2 us  [columns_absorbed(): pl.pallas_call(column_kernel, out_shape=(jax.ShapeDtypeStruct((LEV, SLOTS...]
    unnamed x1 -> x2, local copies, waits for them, and re-layouts: 1.19 us -> 2.59 us
where the time goes in v2:
time: 47.8 us; the launch traced here: 47.6 us
  Pallas kernels  43.2 us (90%)
  local copies, waits for them, and re-layouts  3.81 us (8%)
  between operations  0.64 us (1%)
    pallas_call x1, Pallas kernels, columns_absorbed(): pl.pallas_call(column_kernel, out_shape=(jax.ShapeDtypeStruct((LEV, SLOTS...  43.2 us
    unnamed x2, local copies, waits for them, and re-layouts  2.59 us
    broadcast_in_dim x1, local copies, waits for them, and re-layouts, columns_absorbed(): cosine[None]  1.22 us

profile of v2, /device:TPU:1, one launch (start us, length us, event | category | flops | bytes accessed | tf_op | source)
XLA Modules:
  0.0 47.6 jit_solution(16683647882763791724)
XLA Ops:
  0.6 1.2 %broadcast_in_dim.18.cosine_hbm = bf16[1,256]{1,0:T(2,128)(2,1)} reshape(bf16[256]{0:T(256)(128)(2,1)} %param.10) | data formatting | bytes 1024 | tf_op jit(solution)/shard_map/broadcast_in_dim | solution.py:370
  1.8 43.2 %shard_map.104 = (f32[64,256]{1,0:T(8,128)}, f32[1,64]{1,0:T(1,128)}) custom-call(bf16[256,4096]{1,0:T(8,128)(2,1)} %feat_hbm.1, bf16[1,256]{1,0:T(2,128)(2,1)} %broadcast_in_dim.18.cosine_hbm, bf16[2,256]{1,0:T(2,128)(2,1)} %albedo_hbm.1, s32[1,256]{1,0:T(1,128)} %bitcast.5, s32[1,256]{1,0:T(1,128)} %bitcast.6, bf16[64,224]{1,0:T(8,128)(2,1)} %gas_hbm.1, ...), custom_call_target="tpu_custom_call" | custom-call | flops 200000000 | bytes 2200000 | tf_op jit(solution)/shard_map/pallas_call | solution.py:330
  45.0 1.5 %copy.13 = f32[64,256]{1,0:T(8,128)} copy(f32[64,256]{1,0:T(8,128)} %get-tuple-element.4) | data formatting | bytes 131072
  46.5 1.1 %copy.14 = f32[1,64]{1,0:T(1,128)} copy(f32[1,64]{1,0:T(1,128)} %get-tuple-element.5) | data formatting | bytes 512

commit v3 on v2

v3 whole, which is shorter than its diff:
```python
import functools
import jax
import jax.numpy as jnp
from jax import lax
from jax.sharding import PartitionSpec as P
from jax.experimental import pallas as pl
from jax.experimental.pallas import tpu as pltpu

LEV = 64
NF = 64
G = 112
LANES = 128
SUB = 8
GB = G // SUB
PAIRS = LEV // 2
KINDS = 2
LOG2E = 1.4426950408889634
NT = (((1,), (1,)), ((), ()))
NN = (((1,), (0,)), ((), ()))


def recip(x):
    return pl.reciprocal(x, approx=True)


def mxu(a, b, dims):
    return lax.dot_general(a, b, dims, preferred_element_type=jnp.float32)


def column_kernel(
    feat_hbm, cosine_hbm, albedo_hbm, sunlit_hbm, map_hbm, gas_hbm, asym_hbm, solar_hbm, swap_hbm,
    out_ref, mean_ref,
    feat_ref, cosine_ref, albedo_ref, sunlit_ref, map_ref, gas_ref, asym_ref, solar_ref, swap_ref,
    weight_ref, const_ref, solar_rows_ref, depth_0, depth_1, depth_2, depth_3, depth_4, depth_5, depth_6, depth_7,
    state_ref, gain_ref, add_ref, admit_ref, down_ref, net_ref,
    own_ref, mask_ref, part_ref, other_ref, strip_ref, last_ref,
    small_sem, feat_sem, send_a, recv_a, send_b, recv_b, send_c, recv_c,
):
    f32 = jnp.float32
    bf16 = jnp.bfloat16
    chunks = [
        pltpu.make_async_copy(
            feat_hbm.at[pl.ds(n * LANES, LANES), :], feat_ref.at[pl.ds(n * LANES, LANES), :], feat_sem.at[n]
        )
        for n in range(2)
    ]
    small = [
        pltpu.make_async_copy(src, dst, small_sem.at[n])
        for n, (src, dst) in enumerate(
            (
                (sunlit_hbm, sunlit_ref), (map_hbm, map_ref), (cosine_hbm, cosine_ref),
                (albedo_hbm, albedo_ref), (gas_hbm, gas_ref), (asym_hbm, asym_ref), (solar_hbm, solar_ref),
                (swap_hbm, swap_ref),
            )
        )
    ]
    for copy in small:
        copy.start()
    for copy in chunks:
        copy.start()

    n_lon, n_lat = lax.axis_size("lon"), lax.axis_size("lat")
    lon, lat = lax.axis_index("lon"), lax.axis_index("lat")
    groups = n_lon * n_lat
    chips = groups // 2
    core = lax.rem(lon, 2)
    chip = lax.div(lon, 2) * n_lat + lat
    mesh_ids = pl.DeviceIdType.MESH
    sibling = (lon + 1 - 2 * core, lat)
    peers = [
        (lax.rem(lon + 2 * a, n_lon), lax.rem(lat + c, n_lat))
        for a in range(n_lon // 2) for c in range(n_lat) if a or c
    ]
    barrier = pltpu.get_barrier_semaphore()
    for device in [sibling] + peers:
        pl.semaphore_signal(barrier, inc=1, device_id=device, device_id_type=mesh_ids)

    def remote(src, dst, sends, recvs, n, device):
        return pltpu.make_async_remote_copy(
            src_ref=src, dst_ref=dst, send_sem=sends.at[n], recv_sem=recvs.at[n],
            device_id=device, device_id_type=mesh_ids,
        )

    mask_copies = [
        remote(own_ref.at[0], mask_ref.at[core, chip], send_a, recv_a, n, device)
        for n, device in enumerate(peers)
    ]
    mask_pair = remote(mask_ref.at[core], mask_ref.at[core], send_b, recv_b, 0, sibling)

    for copy in small:
        copy.wait()

    listed = jnp.broadcast_to(swap_ref[...].astype(f32), (LANES, LANES // 2)).T
    lane_no = lax.broadcasted_iota(jnp.int32, (LANES // 2, LANES), 1).astype(f32)
    own_ref[0] = jnp.max(jnp.where(listed == lane_no, 1.0, 0.0), axis=0, keepdims=True)

    table = gas_ref[...]
    stacked = jnp.concatenate([table, table], axis=0)
    row = lax.broadcasted_iota(jnp.int32, (2 * G, 2 * G), 0)
    col = lax.broadcasted_iota(jnp.int32, (2 * G, 2 * G), 1)
    turned = mxu(jnp.where(row == col, 1.0, 0.0).astype(bf16), stacked, NT)

    def to_rows(line):
        return jnp.broadcast_to(line, (LANES, G)).T

    asym = to_rows(asym_ref[...])
    solar_rows_ref[...] = to_rows(solar_ref[...])
    absorb = turned[:G]
    scatter = turned[G:]
    first = lax.broadcasted_iota(jnp.int32, (G, LANES), 1) < NF
    weight_ref[:G, :] = jnp.where(first, 2.0 * absorb, 2.0 * scatter).astype(bf16)
    weight_ref[G:, :] = jnp.where(first, 0.0, 2.0 * scatter).astype(bf16)
    const_ref[0] = 0.245 * (1.0 + 3.0 * asym)
    const_ref[1] = 0.98 * (0.5 - 0.25 * asym)
    const_ref[2] = 0.98 * (0.5 + 0.25 * asym)

    low_lanes = lax.broadcasted_iota(jnp.int32, (LANES, LANES), 1) < NF

    def one_block(block, carry):
        @pl.when(block == 0)
        def _():
            chunks[0].wait()

        @pl.when(block == 1)
        def _():
            chunks[1].wait()
            pl.semaphore_wait(barrier, chips)
            mask_ref[core, chip] = own_ref[0]
            for copy in mask_copies:
                copy.start()

        lanes = pl.ds(pl.multiple_of(block * LANES, LANES), LANES)
        cosine = cosine_ref[:, lanes].astype(f32)
        slant = jnp.broadcast_to((-0.5 * LOG2E) / cosine, (SUB, LANES))
        alb_dir = jnp.broadcast_to(albedo_ref[0:1, lanes].astype(f32), (SUB, LANES))
        alb_dif = jnp.broadcast_to(albedo_ref[1:2, lanes].astype(f32), (SUB, LANES))
        state_ref[0] = solar_rows_ref[...] * (cosine * sunlit_ref[:, lanes].astype(f32))
        state_ref[1] = jnp.ones((G, LANES), f32)
        state_ref[2] = jnp.zeros((G, LANES), f32)
        state_ref[3] = jnp.zeros((G, LANES), f32)

        def optical(pair, depth):
            chunk = feat_ref[lanes, pl.ds(pl.multiple_of(pair * LANES, LANES), LANES)]
            turn = jnp.concatenate([chunk[:, NF:], chunk[:, :NF]], axis=1)
            both = jnp.concatenate(
                [jnp.where(low_lanes, chunk, turn), jnp.where(low_lanes, turn, chunk)], axis=0
            )
            depth[...] = mxu(weight_ref[...], both, NT)

        def one_pair(pair, depth):
            totals = [jnp.zeros((SUB, LANES), f32) for _ in range(2)]
            for g in range(GB):
                rows = pl.ds(g * SUB, SUB)
                direct, admit, source, left = (state_ref[n, rows, :] for n in range(4))
                slope, to_up, to_dn = (const_ref[n, rows, :] for n in range(3))
                for odd in range(2):
                    layer = 2 * pair + odd
                    tau, ray = (
                        depth[n * G + g * SUB : n * G + (g + 1) * SUB, odd * LANES : (odd + 1) * LANES]
                        for n in range(KINDS)
                    )
                    t_one = tau - 0.98 * ray
                    t_two = tau - slope * ray
                    product = t_one * t_two
                    root = lax.rsqrt(product)
                    x = product * root
                    sigma = t_one * root
                    th = jnp.tanh(x)
                    e = jnp.exp2(x * (-LOG2E))
                    sech = e + e * th
                    below = direct * jnp.exp2(tau * slant)
                    lost = (direct - below) * recip(tau) * ray
                    up = to_up * lost
                    dn = to_dn * lost
                    jump = up - left
                    totals[odd] = totals[odd] + (source + direct)
                    inner = source + up - admit * jump
                    z = recip(sigma + admit * th)
                    zs = z * sigma
                    gain = sech * zs
                    gain_ref[layer, rows, :] = gain
                    add_ref[layer, rows, :] = (th * z) * inner + jump
                    admit_ref[layer, rows, :] = admit
                    admit = (admit + sigma * th) * zs
                    source = gain * inner + dn
                    direct = below
                    left = dn
                for n, value in enumerate((direct, admit, source, left)):
                    state_ref[n, rows, :] = value
            for odd in range(2):
                down_ref[2 * pair + odd] = totals[odd]

        optical(0, depth_0)
        optical(1, depth_1)
        optical(2, depth_2)
        optical(3, depth_3)

        def down(step, inner_carry):
            one_pair(8 * step + 0, depth_0)
            one_pair(8 * step + 1, depth_1)
            one_pair(8 * step + 2, depth_2)
            one_pair(8 * step + 3, depth_3)
            optical(8 * step + 4, depth_4)
            optical(8 * step + 5, depth_5)
            optical(8 * step + 6, depth_6)
            optical(8 * step + 7, depth_7)
            one_pair(8 * step + 4, depth_4)
            one_pair(8 * step + 5, depth_5)
            one_pair(8 * step + 6, depth_6)
            one_pair(8 * step + 7, depth_7)
            optical(jnp.minimum(8 * step + 8, PAIRS - 1), depth_0)
            optical(jnp.minimum(8 * step + 9, PAIRS - 1), depth_1)
            optical(jnp.minimum(8 * step + 10, PAIRS - 1), depth_2)
            optical(jnp.minimum(8 * step + 11, PAIRS - 1), depth_3)
            return inner_carry

        lax.fori_loop(0, PAIRS // 8, down, 0)

        @pl.when(block == 1)
        def _():
            for copy in mask_copies:
                copy.wait()
            mask_pair.start()

        fluxes = []
        total = jnp.zeros((SUB, LANES), f32)
        for g in range(GB):
            rows = pl.ds(g * SUB, SUB)
            direct, admit, source, left = (state_ref[n, rows, :] for n in range(4))
            over = source * (1.0 + alb_dif) + 2.0 * alb_dir * direct - left * (1.0 - alb_dif)
            flux = over / ((1.0 - alb_dif) + admit * (1.0 + alb_dif))
            total = total + (direct + source - admit * flux)
            fluxes.append(flux)
        net_ref[LEV : LEV + 1, :] = jnp.sum(total, axis=0, keepdims=True)

        def upward(step, fluxes):
            for odd in range(2):
                layer = LEV - 1 - 2 * step - odd
                total = down_ref[layer]
                out = []
                for g in range(GB):
                    rows = pl.ds(g * SUB, SUB)
                    flux = gain_ref[layer, rows, :] * fluxes[g] + add_ref[layer, rows, :]
                    total = total - admit_ref[layer, rows, :] * flux
                    out.append(flux)
                fluxes = tuple(out)
                net_ref[pl.ds(layer, 1), :] = jnp.sum(total, axis=0, keepdims=True)
            return fluxes

        lax.fori_loop(0, LEV // 2, upward, tuple(fluxes))
        live = map_ref[:, lanes] >= 0
        out_ref[:, lanes] = jnp.where(live, net_ref[0:LEV, :] - net_ref[1 : LEV + 1, :], 0.0)
        return carry

    lax.fori_loop(0, 2, one_block, 0)
    mask_pair.wait()

    place = map_ref[...]
    home = lax.shift_right_arithmetic(place, 7)
    home_core = lax.rem(lax.div(home, n_lat), 2)
    home_chip = lax.div(home, 2 * n_lat) * n_lat + lax.rem(home, n_lat)
    away_chip = jnp.where(home_chip >= chips // 2, home_chip - chips // 2, home_chip + chips // 2)
    slot = place & (LANES - 1)
    slots = place.shape[1]
    group_row = lax.broadcasted_iota(jnp.int32, (groups, slots), 0)
    at_home = jnp.where(home_core * chips + home_chip == group_row, 1.0, 0.0).astype(bf16)
    at_slot = jnp.where(slot == lax.broadcasted_iota(jnp.int32, (LANES, slots), 0), 1.0, 0.0)
    masks = mask_ref[...].reshape(groups, LANES)
    listed_at = mxu(masks.T.astype(bf16), at_home, NN)
    moved = jnp.sum(listed_at * at_slot, axis=0, keepdims=True)
    held = home_core * chips + jnp.where(moved > 0.5, away_chip, home_chip)
    held = jnp.where(place < 0, -1, held)
    member = jnp.where(held == group_row, 1.0, 0.0).astype(bf16)
    absorbed = jnp.concatenate([out_ref[...], jnp.zeros((LANES - LEV, slots), f32)], axis=0)
    high = absorbed.astype(bf16)
    low = (absorbed - high.astype(f32)).astype(bf16)
    part_ref[...] = (mxu(member, high, NT) + mxu(member, low, NT)).reshape(2, chips, LANES)

    copy = remote(part_ref.at[1 - core], other_ref, send_b, recv_b, 1, sibling)
    copy.start()
    copy.wait()
    strip_ref[...] = (part_ref[core] + other_ref[...]).reshape(chips, 1, LANES)
    copies = [
        remote(strip_ref.at[lax.div(device[0], 2) * n_lat + device[1]], last_ref.at[n], send_c, recv_c, n, device)
        for n, device in enumerate(peers)
    ]
    for copy in copies:
        copy.start()
    for copy in copies:
        copy.wait()
    total = strip_ref[chip] + jnp.sum(last_ref[...], axis=0)
    mean_ref[...] = total[:, :LEV] * (1.0 / LANES)


def columns_absorbed(features, cosine, albedo, sunlit, column_map, swap_list, gas_table, asymmetry, solar):
    anywhere = pl.BlockSpec(memory_space=pl.ANY)
    vmem = pl.BlockSpec(memory_space=pltpu.VMEM)
    f32, bf16, i32 = jnp.float32, jnp.bfloat16, jnp.int32
    chips = lax.axis_size("lon") * lax.axis_size("lat") // 2
    dma = pltpu.SemaphoreType.DMA
    return pl.pallas_call(
        column_kernel,
        out_shape=(jax.ShapeDtypeStruct((LEV, 2 * LANES), f32), jax.ShapeDtypeStruct((1, LEV), f32)),
        in_specs=[anywhere] * 9,
        out_specs=(vmem, vmem),
        scratch_shapes=[
            pltpu.VMEM((2 * LANES, LEV * NF), bf16),
            pltpu.VMEM((1, 2 * LANES), bf16),
            pltpu.VMEM((2, 2 * LANES), bf16),
            pltpu.VMEM((1, 2 * LANES), i32),
            pltpu.VMEM((1, 2 * LANES), i32),
            pltpu.VMEM((NF, 2 * G), bf16),
            pltpu.VMEM((1, G), f32),
            pltpu.VMEM((1, G), f32),
            pltpu.VMEM((1, LANES // 2), i32),
            pltpu.VMEM((KINDS * G, LANES), bf16),
            pltpu.VMEM((3, G, LANES), f32),
            pltpu.VMEM((G, LANES), f32),
            pltpu.VMEM((KINDS * G, 2 * LANES), f32),
            pltpu.VMEM((KINDS * G, 2 * LANES), f32),
            pltpu.VMEM((KINDS * G, 2 * LANES), f32),
            pltpu.VMEM((KINDS * G, 2 * LANES), f32),
            pltpu.VMEM((KINDS * G, 2 * LANES), f32),
            pltpu.VMEM((KINDS * G, 2 * LANES), f32),
            pltpu.VMEM((KINDS * G, 2 * LANES), f32),
            pltpu.VMEM((KINDS * G, 2 * LANES), f32),
            pltpu.VMEM((4, G, LANES), f32),
            pltpu.VMEM((LEV, G, LANES), f32),
            pltpu.VMEM((LEV, G, LANES), f32),
            pltpu.VMEM((LEV, G, LANES), f32),
            pltpu.VMEM((LEV, SUB, LANES), f32),
            pltpu.VMEM((LEV + SUB, LANES), f32),
            pltpu.VMEM((1, 1, LANES), f32),
            pltpu.VMEM((2, chips, 1, LANES), f32),
            pltpu.VMEM((2, chips, LANES), f32),
            pltpu.VMEM((chips, LANES), f32),
            pltpu.VMEM((chips, 1, LANES), f32),
            pltpu.VMEM((chips - 1, 1, LANES), f32),
            dma((8,)), dma((2,)), dma((chips,)), dma((chips,)), dma((2,)), dma((2,)), dma((chips,)), dma((chips,)),
        ],
        compiler_params=pltpu.CompilerParams(collective_id=0, has_side_effects=True, vmem_limit_bytes=60 * 1024 * 1024),
        cost_estimate=pl.CostEstimate(flops=200_000_000, bytes_accessed=2_200_000, transcendentals=10_000_000),
    )(features, cosine[None], albedo, sunlit[None], column_map[None], gas_table, asymmetry[None], solar[None], swap_list[None])


def body(
    features, cosine_zenith, albedo, sunlit, column_map, swap_list, gas_table, asymmetry, solar_source
):
    return columns_absorbed(
        features, cosine_zenith, albedo, sunlit, column_map, swap_list, gas_table, asymmetry, solar_source
    )


def solution(mesh):
    both = ("lon", "lat")
    in_specs = (
        P(both, None), P(both), P(None, both), P(both), P(both), P(both), P(), P(), P(),
    )
    out_specs = (P(None, both), P(both, None))
    return jax.shard_map(body, mesh=mesh, in_specs=in_specs, out_specs=out_specs, check_vma=False)
```

time: 47.8 us -> 38.6 us (0.81)
  Pallas kernels: 43.2 us -> 33.9 us
    pallas_call x1, Pallas kernels: 43.2 us -> 33.9 us  [columns_absorbed(): pl.pallas_call(column_kernel, out_shape=(jax.ShapeDtypeStruct((LEV, 2 * L...]
where the time goes in v3:
time: 38.6 us; the launch traced here: 38.4 us
  Pallas kernels  33.9 us (88%)
  local copies, waits for them, and re-layouts  3.81 us (10%)
  between operations  0.64 us (2%)
    pallas_call x1, Pallas kernels, columns_absorbed(): pl.pallas_call(column_kernel, out_shape=(jax.ShapeDtypeStruct((LEV, 2 * L...  33.9 us
    unnamed x2, local copies, waits for them, and re-layouts  2.59 us
    broadcast_in_dim x1, local copies, waits for them, and re-layouts, columns_absorbed(): cosine[None]  1.22 us

profile of v3, /device:TPU:1, one launch (start us, length us, event | category | flops | bytes accessed | tf_op | source)
XLA Modules:
  0.0 38.4 jit_solution(854270072390051122)
XLA Ops:
  0.6 1.2 %broadcast_in_dim.18.cosine_hbm = bf16[1,256]{1,0:T(2,128)(2,1)} reshape(bf16[256]{0:T(256)(128)(2,1)} %param.10) | data formatting | bytes 1024 | tf_op jit(solution)/shard_map/broadcast_in_dim | solution.py:343
  1.8 33.9 %shard_map.104 = (f32[64,256]{1,0:T(8,128)}, f32[1,64]{1,0:T(1,128)}) custom-call(bf16[256,4096]{1,0:T(8,128)(2,1)} %feat_hbm.1, bf16[1,256]{1,0:T(2,128)(2,1)} %broadcast_in_dim.18.cosine_hbm, bf16[2,256]{1,0:T(2,128)(2,1)} %albedo_hbm.1, s32[1,256]{1,0:T(1,128)} %bitcast.5, s32[1,256]{1,0:T(1,128)} %bitcast.6, bf16[64,224]{1,0:T(8,128)(2,1)} %gas_hbm.1, ...), custom_call_target="tpu_custom_call" | custom-call | flops 200000000 | bytes 2200000 | tf_op jit(solution)/shard_map/pallas_call | solution.py:301
  35.8 1.5 %copy.13 = f32[64,256]{1,0:T(8,128)} copy(f32[64,256]{1,0:T(8,128)} %get-tuple-element.4) | data formatting | bytes 131072
  37.3 1.1 %copy.14 = f32[1,64]{1,0:T(1,128)} copy(f32[1,64]{1,0:T(1,128)} %get-tuple-element.5) | data formatting | bytes 512

commit v4 on v3

--- a/solution.py
+++ b/solution.py
@@ -29,12 +29,12 @@
 
 def column_kernel(
     feat_hbm, cosine_hbm, albedo_hbm, sunlit_hbm, map_hbm, gas_hbm, asym_hbm, solar_hbm, swap_hbm,
-    out_ref, mean_ref,
+    out_hbm, mean_ref,
     feat_ref, cosine_ref, albedo_ref, sunlit_ref, map_ref, gas_ref, asym_ref, solar_ref, swap_ref,
     weight_ref, const_ref, solar_rows_ref, depth_0, depth_1, depth_2, depth_3, depth_4, depth_5, depth_6, depth_7,
     state_ref, gain_ref, add_ref, admit_ref, down_ref, net_ref,
-    own_ref, mask_ref, part_ref, other_ref, strip_ref, last_ref,
-    small_sem, feat_sem, send_a, recv_a, send_b, recv_b, send_c, recv_c,
+    wide_ref, result_ref, own_ref, mask_ref, part_ref, other_ref, strip_ref, last_ref,
+    small_sem, feat_sem, out_sem, send_a, recv_a, send_b, recv_b, send_c, recv_c,
 ):
     f32 = jnp.float32
     bf16 = jnp.bfloat16
@@ -54,9 +54,9 @@
             )
         )
     ]
+    for copy in chunks:
+        copy.start()
     for copy in small:
-        copy.start()
-    for copy in chunks:
         copy.start()
 
     n_lon, n_lat = lax.axis_size("lon"), lax.axis_size("lat")
@@ -94,6 +94,7 @@
     lane_no = lax.broadcasted_iota(jnp.int32, (LANES // 2, LANES), 1).astype(f32)
     own_ref[0] = jnp.max(jnp.where(listed == lane_no, 1.0, 0.0), axis=0, keepdims=True)
 
+    wide_ref[...] = jnp.reshape(cosine_ref[...].astype(f32), (1, 2 * LANES))
     table = gas_ref[...]
     stacked = jnp.concatenate([table, table], axis=0)
     row = lax.broadcasted_iota(jnp.int32, (2 * G, 2 * G), 0)
@@ -130,7 +131,7 @@
                 copy.start()
 
         lanes = pl.ds(pl.multiple_of(block * LANES, LANES), LANES)
-        cosine = cosine_ref[:, lanes].astype(f32)
+        cosine = wide_ref[:, lanes]
         slant = jnp.broadcast_to((-0.5 * LOG2E) / cosine, (SUB, LANES))
         alb_dir = jnp.broadcast_to(albedo_ref[0:1, lanes].astype(f32), (SUB, LANES))
         alb_dif = jnp.broadcast_to(albedo_ref[1:2, lanes].astype(f32), (SUB, LANES))
@@ -139,13 +140,19 @@
         state_ref[2] = jnp.zeros((G, LANES), f32)
         state_ref[3] = jnp.zeros((G, LANES), f32)
 
-        def optical(pair, depth):
+        def optical(pair, depth, guard=None):
             chunk = feat_ref[lanes, pl.ds(pl.multiple_of(pair * LANES, LANES), LANES)]
-            turn = jnp.concatenate([chunk[:, NF:], chunk[:, :NF]], axis=1)
+            if guard is not None:
+                chunk = chunk + guard
+            turn = chunk.T
             both = jnp.concatenate(
-                [jnp.where(low_lanes, chunk, turn), jnp.where(low_lanes, turn, chunk)], axis=0
+                [
+                    jnp.concatenate([turn[:NF], turn[:NF]], axis=0),
+                    jnp.concatenate([turn[NF:], turn[NF:]], axis=0),
+                ],
+                axis=1,
             )
-            depth[...] = mxu(weight_ref[...], both, NT)
+            depth[...] = mxu(weight_ref[...], both, NN)
 
         def one_pair(pair, depth):
             totals = [jnp.zeros((SUB, LANES), f32) for _ in range(2)]
@@ -189,6 +196,7 @@
                     state_ref[n, rows, :] = value
             for odd in range(2):
                 down_ref[2 * pair + odd] = totals[odd]
+            return jnp.minimum(th[0:1], 0.0).astype(bf16)
 
         optical(0, depth_0)
         optical(1, depth_1)
@@ -196,22 +204,31 @@
         optical(3, depth_3)
 
         def down(step, inner_carry):
-            one_pair(8 * step + 0, depth_0)
-            one_pair(8 * step + 1, depth_1)
-            one_pair(8 * step + 2, depth_2)
-            one_pair(8 * step + 3, depth_3)
-            optical(8 * step + 4, depth_4)
-            optical(8 * step + 5, depth_5)
-            optical(8 * step + 6, depth_6)
-            optical(8 * step + 7, depth_7)
-            one_pair(8 * step + 4, depth_4)
-            one_pair(8 * step + 5, depth_5)
-            one_pair(8 * step + 6, depth_6)
-            one_pair(8 * step + 7, depth_7)
-            optical(jnp.minimum(8 * step + 8, PAIRS - 1), depth_0)
-            optical(jnp.minimum(8 * step + 9, PAIRS - 1), depth_1)
-            optical(jnp.minimum(8 * step + 10, PAIRS - 1), depth_2)
-            optical(jnp.minimum(8 * step + 11, PAIRS - 1), depth_3)
+            guard = None
+            next_guard = one_pair(8 * step + 0, depth_0)
+            optical(8 * step + 4, depth_4, guard)
+            guard = next_guard
+            next_guard = one_pair(8 * step + 1, depth_1)
+            optical(8 * step + 5, depth_5, guard)
+            guard = next_guard
+            next_guard = one_pair(8 * step + 2, depth_2)
+            optical(8 * step + 6, depth_6, guard)
+            guard = next_guard
+            next_guard = one_pair(8 * step + 3, depth_3)
+            optical(8 * step + 7, depth_7, guard)
+            guard = next_guard
+            next_guard = one_pair(8 * step + 4, depth_4)
+            optical(jnp.minimum(8 * step + 8, PAIRS - 1), depth_0, guard)
+            guard = next_guard
+            next_guard = one_pair(8 * step + 5, depth_5)
+            optical(jnp.minimum(8 * step + 9, PAIRS - 1), depth_1, guard)
+            guard = next_guard
+            next_guard = one_pair(8 * step + 6, depth_6)
+            optical(jnp.minimum(8 * step + 10, PAIRS - 1), depth_2, guard)
+            guard = next_guard
+            next_guard = one_pair(8 * step + 7, depth_7)
+            optical(jnp.minimum(8 * step + 11, PAIRS - 1), depth_3, guard)
+            guard = next_guard
             return inner_carry
 
         lax.fori_loop(0, PAIRS // 8, down, 0)
@@ -234,8 +251,8 @@
         net_ref[LEV : LEV + 1, :] = jnp.sum(total, axis=0, keepdims=True)
 
         def upward(step, fluxes):
-            for odd in range(2):
-                layer = LEV - 1 - 2 * step - odd
+            for odd in range(4):
+                layer = LEV - 1 - 4 * step - odd
                 total = down_ref[layer]
                 out = []
                 for g in range(GB):
@@ -247,12 +264,14 @@
                 net_ref[pl.ds(layer, 1), :] = jnp.sum(total, axis=0, keepdims=True)
             return fluxes
 
-        lax.fori_loop(0, LEV // 2, upward, tuple(fluxes))
+        lax.fori_loop(0, LEV // 4, upward, tuple(fluxes))
         live = map_ref[:, lanes] >= 0
-        out_ref[:, lanes] = jnp.where(live, net_ref[0:LEV, :] - net_ref[1 : LEV + 1, :], 0.0)
+        result_ref[:, lanes] = jnp.where(live, net_ref[0:LEV, :] - net_ref[1 : LEV + 1, :], 0.0)
         return carry
 
     lax.fori_loop(0, 2, one_block, 0)
+    out_copy = pltpu.make_async_copy(result_ref, out_hbm, out_sem.at[0])
+    out_copy.start()
     mask_pair.wait()
 
     place = map_ref[...]
@@ -271,7 +290,7 @@
     held = home_core * chips + jnp.where(moved > 0.5, away_chip, home_chip)
     held = jnp.where(place < 0, -1, held)
     member = jnp.where(held == group_row, 1.0, 0.0).astype(bf16)
-    absorbed = jnp.concatenate([out_ref[...], jnp.zeros((LANES - LEV, slots), f32)], axis=0)
+    absorbed = jnp.concatenate([result_ref[...], jnp.zeros((LANES - LEV, slots), f32)], axis=0)
     high = absorbed.astype(bf16)
     low = (absorbed - high.astype(f32)).astype(bf16)
     part_ref[...] = (mxu(member, high, NT) + mxu(member, low, NT)).reshape(2, chips, LANES)
@@ -290,6 +309,7 @@
         copy.wait()
     total = strip_ref[chip] + jnp.sum(last_ref[...], axis=0)
     mean_ref[...] = total[:, :LEV] * (1.0 / LANES)
+    out_copy.wait()
 
 
 def columns_absorbed(features, cosine, albedo, sunlit, column_map, swap_list, gas_table, asymmetry, solar):
@@ -302,10 +322,10 @@
         column_kernel,
         out_shape=(jax.ShapeDtypeStruct((LEV, 2 * LANES), f32), jax.ShapeDtypeStruct((1, LEV), f32)),
         in_specs=[anywhere] * 9,
-        out_specs=(vmem, vmem),
+        out_specs=(anywhere, vmem),
         scratch_shapes=[
             pltpu.VMEM((2 * LANES, LEV * NF), bf16),
-            pltpu.VMEM((1, 2 * LANES), bf16),
+            pltpu.VMEM((2 * LANES,), bf16),
             pltpu.VMEM((2, 2 * LANES), bf16),
             pltpu.VMEM((1, 2 * LANES), i32),
             pltpu.VMEM((1, 2 * LANES), i32),
@@ -330,25 +350,53 @@
             pltpu.VMEM((LEV, G, LANES), f32),
             pltpu.VMEM((LEV, SUB, LANES), f32),
             pltpu.VMEM((LEV + SUB, LANES), f32),
+            pltpu.VMEM((1, 2 * LANES), f32),
+            pltpu.VMEM((LEV, 2 * LANES), f32),
             pltpu.VMEM((1, 1, LANES), f32),
             pltpu.VMEM((2, chips, 1, LANES), f32),
             pltpu.VMEM((2, chips, LANES), f32),
             pltpu.VMEM((chips, LANES), f32),
             pltpu.VMEM((chips, 1, LANES), f32),
             pltpu.VMEM((chips - 1, 1, LANES), f32),
-            dma((8,)), dma((2,)), dma((chips,)), dma((chips,)), dma((2,)), dma((2,)), dma((chips,)), dma((chips,)),
+            dma((8,)), dma((2,)), dma((2,)), dma((chips,)), dma((chips,)), dma((2,)), dma((2,)), dma((chips,)), dma((chips,)),
         ],
         compiler_params=pltpu.CompilerParams(collective_id=0, has_side_effects=True, vmem_limit_bytes=60 * 1024 * 1024),
         cost_estimate=pl.CostEstimate(flops=200_000_000, bytes_accessed=2_200_000, transcendentals=10_000_000),
-    )(features, cosine[None], albedo, sunlit[None], column_map[None], gas_table, asymmetry[None], solar[None], swap_list[None])
+    )(features, cosine, albedo, sunlit[None], column_map[None], gas_table, asymmetry[None], solar[None], swap_list[None])
+
+
+def finish_kernel(absorbed_hbm, mean_hbm, absorbed_out, mean_out, sems):
+    copies = [
+        pltpu.make_async_copy(absorbed_hbm, absorbed_out, sems.at[0]),
+        pltpu.make_async_copy(mean_hbm, mean_out, sems.at[1]),
+    ]
+    for copy in copies:
+        copy.start()
+    for copy in copies:
+        copy.wait()
+
+
+def finished(absorbed, mean):
+    anywhere = pl.BlockSpec(memory_space=pl.ANY)
+    return pl.pallas_call(
+        finish_kernel,
+        out_shape=(
+            jax.ShapeDtypeStruct(absorbed.shape, absorbed.dtype), jax.ShapeDtypeStruct(mean.shape, mean.dtype)
+        ),
+        in_specs=[anywhere] * 2,
+        out_specs=(anywhere, anywhere),
+        scratch_shapes=[pltpu.SemaphoreType.DMA((2,))],
+        compiler_params=pltpu.CompilerParams(vmem_limit_bytes=60 * 1024 * 1024),
+    )(absorbed, mean)
 
 
 def body(
     features, cosine_zenith, albedo, sunlit, column_map, swap_list, gas_table, asymmetry, solar_source
 ):
-    return columns_absorbed(
+    absorbed, mean = columns_absorbed(
         features, cosine_zenith, albedo, sunlit, column_map, swap_list, gas_table, asymmetry, solar_source
     )
+    return finished(absorbed, mean)
 
 
 def solution(mesh):

time: 38.6 us -> 37 us (0.959)
  local copies, waits for them, and re-layouts: 3.81 us -> 0 us
  Pallas kernels: 33.9 us -> 36.2 us
    pallas_call x0 -> x1, Pallas kernels: none -> 3.12 us  [finished(): pl.pallas_call(finish_kernel, out_shape=(jax.ShapeDtypeStruct(absorbed.sh...]
    unnamed x2 -> x0, local copies, waits for them, and re-layouts: 2.59 us -> none
    broadcast_in_dim x1 -> x0, local copies, waits for them, and re-layouts: 1.22 us -> none  [columns_absorbed(): cosine[None]]
    pallas_call x1, Pallas kernels: 33.9 us -> 33.1 us  [columns_absorbed(): pl.pallas_call(column_kernel, out_shape=(jax.ShapeDtypeStruct((LEV, 2 * L...]
where the time goes in v4:
time: 37 us; the launch traced here: 36.8 us
  Pallas kernels  36.2 us (98%)
  between operations  0.64 us (2%)
    pallas_call x1, Pallas kernels, columns_absorbed(): pl.pallas_call(column_kernel, out_shape=(jax.ShapeDtypeStruct((LEV, 2 * L...  33.1 us
    pallas_call x1, Pallas kernels, finished(): pl.pallas_call(finish_kernel, out_shape=(jax.ShapeDtypeStruct(absorbed.sh...  3.12 us

profile of v4, /device:TPU:1, one launch (start us, length us, event | category | flops | bytes accessed | tf_op | source)
XLA Modules:
  0.0 36.8 jit_solution(18017276973781865620)
XLA Ops:
  0.6 33.1 %shard_map.104 = (f32[64,256]{1,0:T(8,128)}, f32[1,64]{1,0:T(1,128)}) custom-call(bf16[256,4096]{1,0:T(8,128)(2,1)} %feat_hbm.1, bf16[256]{0:T(256)(128)(2,1)} %cosine_hbm.1, bf16[2,256]{1,0:T(2,128)(2,1)} %albedo_hbm.1, s32[1,256]{1,0:T(1,128)} %bitcast.5, s32[1,256]{1,0:T(1,128)} %bitcast.6, bf16[64,224]{1,0:T(8,128)(2,1)} %gas_hbm.1, f32[1,112]{1,0:T(1,128)} %bitcast.7, ...), custom_call_target="tpu_custom_call" | custom-call | flops 200000000 | bytes 2200000 | tf_op jit(solution)/shard_map/pallas_call | solution.py:321
  33.7 3.1 %shard_map.105 = (f32[64,256]{1,0:T(8,128)}, f32[1,64]{1,0:T(1,128)}) custom-call(f32[64,256]{1,0:T(8,128)} %get-tuple-element.4.absorbed_hbm, f32[1,64]{1,0:T(1,128)} %get-tuple-element.5.mean_hbm), custom_call_target="tpu_custom_call" | custom-call | tf_op jit(solution)/shard_map/pallas_call | solution.py:381

commit v5 on v4

--- a/solution.py
+++ b/solution.py
@@ -29,7 +29,7 @@
 
 def column_kernel(
     feat_hbm, cosine_hbm, albedo_hbm, sunlit_hbm, map_hbm, gas_hbm, asym_hbm, solar_hbm, swap_hbm,
-    out_hbm, mean_ref,
+    out_hbm, sum_ref,
     feat_ref, cosine_ref, albedo_ref, sunlit_ref, map_ref, gas_ref, asym_ref, solar_ref, swap_ref,
     weight_ref, const_ref, solar_rows_ref, depth_0, depth_1, depth_2, depth_3, depth_4, depth_5, depth_6, depth_7,
     state_ref, gain_ref, add_ref, admit_ref, down_ref, net_ref,
@@ -265,8 +265,7 @@
             return fluxes
 
         lax.fori_loop(0, LEV // 4, upward, tuple(fluxes))
-        live = map_ref[:, lanes] >= 0
-        result_ref[:, lanes] = jnp.where(live, net_ref[0:LEV, :] - net_ref[1 : LEV + 1, :], 0.0)
+        result_ref[:, lanes] = net_ref[0:LEV, :] - net_ref[1 : LEV + 1, :]
         return carry
 
     lax.fori_loop(0, 2, one_block, 0)
@@ -290,7 +289,8 @@
     held = home_core * chips + jnp.where(moved > 0.5, away_chip, home_chip)
     held = jnp.where(place < 0, -1, held)
     member = jnp.where(held == group_row, 1.0, 0.0).astype(bf16)
-    absorbed = jnp.concatenate([result_ref[...], jnp.zeros((LANES - LEV, slots), f32)], axis=0)
+    absorbed = jnp.where(place < 0, 0.0, result_ref[...])
+    absorbed = jnp.concatenate([absorbed, jnp.zeros((LANES - LEV, slots), f32)], axis=0)
     high = absorbed.astype(bf16)
     low = (absorbed - high.astype(f32)).astype(bf16)
     part_ref[...] = (mxu(member, high, NT) + mxu(member, low, NT)).reshape(2, chips, LANES)
@@ -308,7 +308,7 @@
     for copy in copies:
         copy.wait()
     total = strip_ref[chip] + jnp.sum(last_ref[...], axis=0)
-    mean_ref[...] = total[:, :LEV] * (1.0 / LANES)
+    sum_ref[...] = total[:, :LEV]
     out_copy.wait()
 
 
@@ -364,39 +364,14 @@
         cost_estimate=pl.CostEstimate(flops=200_000_000, bytes_accessed=2_200_000, transcendentals=10_000_000),
     )(features, cosine, albedo, sunlit[None], column_map[None], gas_table, asymmetry[None], solar[None], swap_list[None])
 
-
-def finish_kernel(absorbed_hbm, mean_hbm, absorbed_out, mean_out, sems):
-    copies = [
-        pltpu.make_async_copy(absorbed_hbm, absorbed_out, sems.at[0]),
-        pltpu.make_async_copy(mean_hbm, mean_out, sems.at[1]),
-    ]
-    for copy in copies:
-        copy.start()
-    for copy in copies:
-        copy.wait()
-
-
-def finished(absorbed, mean):
-    anywhere = pl.BlockSpec(memory_space=pl.ANY)
-    return pl.pallas_call(
-        finish_kernel,
-        out_shape=(
-            jax.ShapeDtypeStruct(absorbed.shape, absorbed.dtype), jax.ShapeDtypeStruct(mean.shape, mean.dtype)
-        ),
-        in_specs=[anywhere] * 2,
-        out_specs=(anywhere, anywhere),
-        scratch_shapes=[pltpu.SemaphoreType.DMA((2,))],
-        compiler_params=pltpu.CompilerParams(vmem_limit_bytes=60 * 1024 * 1024),
-    )(absorbed, mean)
-
-
 def body(
     features, cosine_zenith, albedo, sunlit, column_map, swap_list, gas_table, asymmetry, solar_source
 ):
-    absorbed, mean = columns_absorbed(
+    absorbed, sums = columns_absorbed(
         features, cosine_zenith, albedo, sunlit, column_map, swap_list, gas_table, asymmetry, solar_source
     )
-    return finished(absorbed, mean)
+    live = column_map[None] >= 0
+    return jnp.where(live, absorbed, 0.0), sums * (1.0 / LANES)
 
 
 def solution(mesh):

time: 37 us -> 37.1 us (level)
  other arithmetic: 0 us -> 3.28 us
  Pallas kernels: 36.2 us -> 33 us
    pallas_call x1 -> x0, Pallas kernels: 3.12 us -> none  [finished(): pl.pallas_call(finish_kernel, out_shape=(jax.ShapeDtypeStruct(absorbed.sh...]
    select_n x0 -> x1, other arithmetic: none -> 1.48 us  [body(): return (jnp.where(live, absorbed, 0.0), sums * (1.0 / LANES))]
    mul x0 -> x1, other arithmetic: none -> 1.12 us  [body(): return (jnp.where(live, absorbed, 0.0), sums * (1.0 / LANES))]
    ge x0 -> x1, other arithmetic: none -> 0.69 us  [body(): live = column_map[None] >= 0]
where the time goes in v5:
time: 37.1 us; the launch traced here: 36.9 us
  Pallas kernels  33 us (89%)
  other arithmetic  3.28 us (9%)
  between operations  0.64 us (2%)
    pallas_call x1, Pallas kernels, columns_absorbed(): pl.pallas_call(column_kernel, out_shape=(jax.ShapeDtypeStruct((LEV, 2 * L...  33 us
    select_n x1, other arithmetic, body(): return (jnp.where(live, absorbed, 0.0), sums * (1.0 / LANES))  1.48 us
    mul x1, other arithmetic, body(): return (jnp.where(live, absorbed, 0.0), sums * (1.0 / LANES))  1.12 us

profile of v5, /device:TPU:1, one launch (start us, length us, event | category | flops | bytes accessed | tf_op | source)
XLA Modules:
  0.0 36.9 jit_solution(15069931784471190221)
XLA Ops:
  0.6 0.7 %broadcast_compare_fusion = pred[256]{0:T(512)(128)(4,1)S(1)} fusion(s32[256]{0:T(256)} %param.13), kind=kLoop, calls=%fused_computation.1 | loop fusion | flops 256 | bytes 1280 | tf_op jit(solution)/shard_map/ge | solution.py:373
  1.3 33.0 %shard_map.104 = (f32[64,256]{1,0:T(8,128)}, f32[1,64]{1,0:T(1,128)}) custom-call(bf16[256,4096]{1,0:T(8,128)(2,1)} %feat_hbm.1, bf16[256]{0:T(256)(128)(2,1)} %cosine_hbm.1, bf16[2,256]{1,0:T(2,128)(2,1)} %albedo_hbm.1, s32[1,256]{1,0:T(1,128)} %bitcast.5, s32[1,256]{1,0:T(1,128)} %bitcast.6, bf16[64,224]{1,0:T(8,128)(2,1)} %gas_hbm.1, f32[1,112]{1,0:T(1,128)} %bitcast.7, ...), custom_call_target="tpu_custom_call" | custom-call | flops 200000000 | bytes 2200000 | tf_op jit(solution)/shard_map/pallas_call | solution.py:321
  34.3 1.5 %broadcast_select_fusion = f32[64,256]{1,0:T(8,128)} fusion(f32[64,256]{1,0:T(8,128)} %get-tuple-element.4, pred[256]{0:T(512)(128)(4,1)S(1)} %broadcast_compare_fusion), kind=kLoop, calls=%fused_computation | loop fusion | flops 16384 | bytes 131328 | tf_op jit(solution)/shard_map/jit(_where)/select_n | solution.py:374
  35.8 1.1 %broadcast_multiply_fusion = f32[1,64]{1,0:T(1,128)} fusion(f32[1,64]{1,0:T(1,128)} %get-tuple-element.5), kind=kLoop, calls=%fused_computation.2 | loop fusion | flops 64 | bytes 512 | tf_op jit(solution)/shard_map/mul | solution.py:374

commit v6 on v5

--- a/solution.py
+++ b/solution.py
@@ -29,11 +29,11 @@
 
 def column_kernel(
     feat_hbm, cosine_hbm, albedo_hbm, sunlit_hbm, map_hbm, gas_hbm, asym_hbm, solar_hbm, swap_hbm,
-    out_hbm, sum_ref,
+    out_hbm, mean_ref,
     feat_ref, cosine_ref, albedo_ref, sunlit_ref, map_ref, gas_ref, asym_ref, solar_ref, swap_ref,
     weight_ref, const_ref, solar_rows_ref, depth_0, depth_1, depth_2, depth_3, depth_4, depth_5, depth_6, depth_7,
     state_ref, gain_ref, add_ref, admit_ref, down_ref, net_ref,
-    wide_ref, result_ref, own_ref, mask_ref, part_ref, other_ref, strip_ref, last_ref,
+    wide_ref, result_ref, member_ref, own_ref, mask_ref, part_ref, other_ref, strip_ref, last_ref,
     small_sem, feat_sem, out_sem, send_a, recv_a, send_b, recv_b, send_c, recv_c,
 ):
     f32 = jnp.float32
@@ -67,9 +67,21 @@
     chip = lax.div(lon, 2) * n_lat + lat
     mesh_ids = pl.DeviceIdType.MESH
     sibling = (lon + 1 - 2 * core, lat)
+    n_x, n_z = n_lon // 4, n_lat // 2
+    steps = [
+        (dx, high, dz, low_bit)
+        for dx in range(n_x) for high in range(2) for dz in range(n_z) for low_bit in range(2)
+        if dx or high or dz or low_bit
+    ]
+    steps.sort(key=lambda d: -(min(d[0], n_x - d[0]) + min(d[2], n_z - d[2]) + (1 if d[3] else 2 * d[1])))
+    x, y_high = lax.div(lon, 4), lax.rem(lax.div(lon, 2), 2)
+    z, y_low = lax.div(lat, 2), lax.rem(lat, 2)
     peers = [
-        (lax.rem(lon + 2 * a, n_lon), lax.rem(lat + c, n_lat))
-        for a in range(n_lon // 2) for c in range(n_lat) if a or c
+        (
+            lax.rem(x + dx, n_x) * 4 + lax.rem(y_high + high, 2) * 2 + core,
+            lax.rem(z + dz, n_z) * 2 + lax.rem(y_low + low_bit, 2),
+        )
+        for dx, high, dz, low_bit in steps
     ]
     barrier = pltpu.get_barrier_semaphore()
     for device in [sibling] + peers:
@@ -125,10 +137,6 @@
         @pl.when(block == 1)
         def _():
             chunks[1].wait()
-            pl.semaphore_wait(barrier, chips)
-            mask_ref[core, chip] = own_ref[0]
-            for copy in mask_copies:
-                copy.start()
 
         lanes = pl.ds(pl.multiple_of(block * LANES, LANES), LANES)
         cosine = wide_ref[:, lanes]
@@ -204,6 +212,19 @@
         optical(3, depth_3)
 
         def down(step, inner_carry):
+            @pl.when((block == 0) & (step == PAIRS // 8 - 1))
+            def _():
+                pl.semaphore_wait(barrier, chips)
+                mask_ref[core, chip] = own_ref[0]
+                for copy in mask_copies:
+                    copy.start()
+
+            @pl.when((block == 1) & (step == PAIRS // 8 - 1))
+            def _():
+                for copy in mask_copies:
+                    copy.wait()
+                mask_pair.start()
+
             guard = None
             next_guard = one_pair(8 * step + 0, depth_0)
             optical(8 * step + 4, depth_4, guard)
@@ -235,9 +256,24 @@
 
         @pl.when(block == 1)
         def _():
-            for copy in mask_copies:
-                copy.wait()
-            mask_pair.start()
+            mask_pair.wait()
+
+            place = map_ref[...]
+            home = lax.shift_right_arithmetic(place, 7)
+            home_core = lax.rem(lax.div(home, n_lat), 2)
+            home_chip = lax.div(home, 2 * n_lat) * n_lat + lax.rem(home, n_lat)
+            away_chip = jnp.where(home_chip >= chips // 2, home_chip - chips // 2, home_chip + chips // 2)
+            slot = place & (LANES - 1)
+            slots = place.shape[1]
+            group_row = lax.broadcasted_iota(jnp.int32, (groups, slots), 0)
+            at_home = jnp.where(home_core * chips + home_chip == group_row, 1.0, 0.0).astype(bf16)
+            at_slot = jnp.where(slot == lax.broadcasted_iota(jnp.int32, (LANES, slots), 0), 1.0, 0.0)
+            masks = mask_ref[...].reshape(groups, LANES)
+            listed_at = mxu(masks.T.astype(bf16), at_home, NN)
+            moved = jnp.sum(listed_at * at_slot, axis=0, keepdims=True)
+            held = home_core * chips + jnp.where(moved > 0.5, away_chip, home_chip)
+            held = jnp.where(place < 0, -1, held)
+            member_ref[...] = jnp.where(held == group_row, 1.0, 0.0).astype(bf16)
 
         fluxes = []
         total = jnp.zeros((SUB, LANES), f32)
@@ -265,32 +301,17 @@
             return fluxes
 
         lax.fori_loop(0, LEV // 4, upward, tuple(fluxes))
-        result_ref[:, lanes] = net_ref[0:LEV, :] - net_ref[1 : LEV + 1, :]
+        live = map_ref[:, lanes] >= 0
+        result_ref[:, lanes] = jnp.where(live, net_ref[0:LEV, :] - net_ref[1 : LEV + 1, :], 0.0)
         return carry
 
     lax.fori_loop(0, 2, one_block, 0)
     out_copy = pltpu.make_async_copy(result_ref, out_hbm, out_sem.at[0])
     out_copy.start()
-    mask_pair.wait()
-
-    place = map_ref[...]
-    home = lax.shift_right_arithmetic(place, 7)
-    home_core = lax.rem(lax.div(home, n_lat), 2)
-    home_chip = lax.div(home, 2 * n_lat) * n_lat + lax.rem(home, n_lat)
-    away_chip = jnp.where(home_chip >= chips // 2, home_chip - chips // 2, home_chip + chips // 2)
-    slot = place & (LANES - 1)
-    slots = place.shape[1]
-    group_row = lax.broadcasted_iota(jnp.int32, (groups, slots), 0)
-    at_home = jnp.where(home_core * chips + home_chip == group_row, 1.0, 0.0).astype(bf16)
-    at_slot = jnp.where(slot == lax.broadcasted_iota(jnp.int32, (LANES, slots), 0), 1.0, 0.0)
-    masks = mask_ref[...].reshape(groups, LANES)
-    listed_at = mxu(masks.T.astype(bf16), at_home, NN)
-    moved = jnp.sum(listed_at * at_slot, axis=0, keepdims=True)
-    held = home_core * chips + jnp.where(moved > 0.5, away_chip, home_chip)
-    held = jnp.where(place < 0, -1, held)
-    member = jnp.where(held == group_row, 1.0, 0.0).astype(bf16)
-    absorbed = jnp.where(place < 0, 0.0, result_ref[...])
-    absorbed = jnp.concatenate([absorbed, jnp.zeros((LANES - LEV, slots), f32)], axis=0)
+
+    member = member_ref[...]
+    slots = member.shape[1]
+    absorbed = jnp.concatenate([result_ref[...], jnp.zeros((LANES - LEV, slots), f32)], axis=0)
     high = absorbed.astype(bf16)
     low = (absorbed - high.astype(f32)).astype(bf16)
     part_ref[...] = (mxu(member, high, NT) + mxu(member, low, NT)).reshape(2, chips, LANES)
@@ -308,7 +329,7 @@
     for copy in copies:
         copy.wait()
     total = strip_ref[chip] + jnp.sum(last_ref[...], axis=0)
-    sum_ref[...] = total[:, :LEV]
+    mean_ref[...] = total[:, :LEV] * (1.0 / LANES)
     out_copy.wait()
 
 
@@ -352,6 +373,7 @@
             pltpu.VMEM((LEV + SUB, LANES), f32),
             pltpu.VMEM((1, 2 * LANES), f32),
             pltpu.VMEM((LEV, 2 * LANES), f32),
+            pltpu.VMEM((2 * chips, 2 * LANES), bf16),
             pltpu.VMEM((1, 1, LANES), f32),
             pltpu.VMEM((2, chips, 1, LANES), f32),
             pltpu.VMEM((2, chips, LANES), f32),
@@ -367,11 +389,9 @@
 def body(
     features, cosine_zenith, albedo, sunlit, column_map, swap_list, gas_table, asymmetry, solar_source
 ):
-    absorbed, sums = columns_absorbed(
+    return columns_absorbed(
         features, cosine_zenith, albedo, sunlit, column_map, swap_list, gas_table, asymmetry, solar_source
     )
-    live = column_map[None] >= 0
-    return jnp.where(live, absorbed, 0.0), sums * (1.0 / LANES)
 
 
 def solution(mesh):

time: 37.1 us -> 36.5 us (0.984)
  other arithmetic: 3.28 us -> 0 us
  local copies, waits for them, and re-layouts: 0 us -> 2.59 us
    unnamed x0 -> x2, local copies, waits for them, and re-layouts: none -> 2.59 us
    select_n x1 -> x0, other arithmetic: 1.48 us -> none  [body(): return (jnp.where(live, absorbed, 0.0), sums * (1.0 / LANES))]
    mul x1 -> x0, other arithmetic: 1.12 us -> none  [body(): return (jnp.where(live, absorbed, 0.0), sums * (1.0 / LANES))]
    ge x1 -> x0, other arithmetic: 0.69 us -> none  [body(): live = column_map[None] >= 0]
where the time goes in v6:
time: 36.5 us; the launch traced here: 36.4 us
  Pallas kernels  33.1 us (91%)
  local copies, waits for them, and re-layouts  2.59 us (7%)
  between operations  0.64 us (2%)
    pallas_call x1, Pallas kernels, columns_absorbed(): pl.pallas_call(column_kernel, out_shape=(jax.ShapeDtypeStruct((LEV, 2 * L...  33.1 us
    unnamed x2, local copies, waits for them, and re-layouts  2.59 us

profile of v6, /device:TPU:1, one launch (start us, length us, event | category | flops | bytes accessed | tf_op | source)
XLA Modules:
  0.0 36.4 jit_solution(8948354758949625768)
XLA Ops:
  0.6 33.1 %shard_map.104 = (f32[64,256]{1,0:T(8,128)}, f32[1,64]{1,0:T(1,128)}) custom-call(bf16[256,4096]{1,0:T(8,128)(2,1)} %feat_hbm.1, bf16[256]{0:T(256)(128)(2,1)} %cosine_hbm.1, bf16[2,256]{1,0:T(2,128)(2,1)} %albedo_hbm.1, s32[1,256]{1,0:T(1,128)} %bitcast.5, s32[1,256]{1,0:T(1,128)} %bitcast.6, bf16[64,224]{1,0:T(8,128)(2,1)} %gas_hbm.1, f32[1,112]{1,0:T(1,128)} %bitcast.7, ...), custom_call_target="tpu_custom_call" | custom-call | flops 200000000 | bytes 2200000 | tf_op jit(solution)/shard_map/pallas_call | solution.py:342
  33.8 1.5 %copy.13 = f32[64,256]{1,0:T(8,128)} copy(f32[64,256]{1,0:T(8,128)} %get-tuple-element.4) | data formatting | bytes 131072
  35.2 1.1 %copy.14 = f32[1,64]{1,0:T(1,128)} copy(f32[1,64]{1,0:T(1,128)} %get-tuple-element.5) | data formatting | bytes 512

commit v7 on v6

--- a/solution.py
+++ b/solution.py
@@ -29,12 +29,12 @@
 
 def column_kernel(
     feat_hbm, cosine_hbm, albedo_hbm, sunlit_hbm, map_hbm, gas_hbm, asym_hbm, solar_hbm, swap_hbm,
-    out_hbm, mean_ref,
+    result_ref, mean_ref,
     feat_ref, cosine_ref, albedo_ref, sunlit_ref, map_ref, gas_ref, asym_ref, solar_ref, swap_ref,
     weight_ref, const_ref, solar_rows_ref, depth_0, depth_1, depth_2, depth_3, depth_4, depth_5, depth_6, depth_7,
     state_ref, gain_ref, add_ref, admit_ref, down_ref, net_ref,
-    wide_ref, result_ref, member_ref, own_ref, mask_ref, part_ref, other_ref, strip_ref, last_ref,
-    small_sem, feat_sem, out_sem, send_a, recv_a, send_b, recv_b, send_c, recv_c,
+    wide_ref, member_ref, own_ref, mask_ref, part_ref, other_ref, strip_ref, last_ref,
+    small_sem, feat_sem, send_a, recv_a, send_b, recv_b, send_c, recv_c,
 ):
     f32 = jnp.float32
     bf16 = jnp.bfloat16
@@ -306,8 +306,6 @@
         return carry
 
     lax.fori_loop(0, 2, one_block, 0)
-    out_copy = pltpu.make_async_copy(result_ref, out_hbm, out_sem.at[0])
-    out_copy.start()
 
     member = member_ref[...]
     slots = member.shape[1]
@@ -330,7 +328,6 @@
         copy.wait()
     total = strip_ref[chip] + jnp.sum(last_ref[...], axis=0)
     mean_ref[...] = total[:, :LEV] * (1.0 / LANES)
-    out_copy.wait()
 
 
 def columns_absorbed(features, cosine, albedo, sunlit, column_map, swap_list, gas_table, asymmetry, solar):
@@ -341,9 +338,9 @@
     dma = pltpu.SemaphoreType.DMA
     return pl.pallas_call(
         column_kernel,
-        out_shape=(jax.ShapeDtypeStruct((LEV, 2 * LANES), f32), jax.ShapeDtypeStruct((1, LEV), f32)),
+        out_shape=(pltpu.VMEM((LEV, 2 * LANES), f32), pltpu.VMEM((1, LEV), f32)),
         in_specs=[anywhere] * 9,
-        out_specs=(anywhere, vmem),
+        out_specs=(vmem, vmem),
         scratch_shapes=[
             pltpu.VMEM((2 * LANES, LEV * NF), bf16),
             pltpu.VMEM((2 * LANES,), bf16),
@@ -372,7 +369,6 @@
             pltpu.VMEM((LEV, SUB, LANES), f32),
             pltpu.VMEM((LEV + SUB, LANES), f32),
             pltpu.VMEM((1, 2 * LANES), f32),
-            pltpu.VMEM((LEV, 2 * LANES), f32),
             pltpu.VMEM((2 * chips, 2 * LANES), bf16),
             pltpu.VMEM((1, 1, LANES), f32),
             pltpu.VMEM((2, chips, 1, LANES), f32),
@@ -380,7 +376,7 @@
             pltpu.VMEM((chips, LANES), f32),
             pltpu.VMEM((chips, 1, LANES), f32),
             pltpu.VMEM((chips - 1, 1, LANES), f32),
-            dma((8,)), dma((2,)), dma((2,)), dma((chips,)), dma((chips,)), dma((2,)), dma((2,)), dma((chips,)), dma((chips,)),
+            dma((8,)), dma((2,)), dma((chips,)), dma((chips,)), dma((2,)), dma((2,)), dma((chips,)), dma((chips,)),
         ],
         compiler_params=pltpu.CompilerParams(collective_id=0, has_side_effects=True, vmem_limit_bytes=60 * 1024 * 1024),
         cost_estimate=pl.CostEstimate(flops=200_000_000, bytes_accessed=2_200_000, transcendentals=10_000_000),

time: 36.5 us -> 34.4 us (0.942)
  local copies, waits for them, and re-layouts: 2.59 us -> 1.14 us
  Pallas kernels: 33.1 us -> 32.5 us
    unnamed x2, local copies, waits for them, and re-layouts: 2.59 us -> 1.14 us
    pallas_call x1, Pallas kernels: 33.1 us -> 32.5 us  [columns_absorbed(): pl.pallas_call(column_kernel, out_shape=(pltpu.VMEM((LEV, 2 * LANES), f32...]
where the time goes in v7:
time: 34.4 us; the launch traced here: 34.3 us
  Pallas kernels  32.5 us (94%)
  local copies, waits for them, and re-layouts  1.14 us (3%)
  between operations  0.64 us (2%)
    pallas_call x1, Pallas kernels, columns_absorbed(): pl.pallas_call(column_kernel, out_shape=(pltpu.VMEM((LEV, 2 * LANES), f32...  32.5 us
    unnamed x2, local copies, waits for them, and re-layouts  1.14 us

profile of v7, /device:TPU:1, one launch (start us, length us, event | category | flops | bytes accessed | tf_op | source)
XLA Modules:
  0.0 34.3 jit_solution(7830509911010021131)
XLA Ops:
  0.6 32.5 %shard_map.104 = (f32[64,256]{1,0:T(8,128)S(1)}, f32[1,64]{1,0:T(1,128)S(1)}) custom-call(bf16[256,4096]{1,0:T(8,128)(2,1)} %feat_hbm.1, bf16[256]{0:T(256)(128)(2,1)} %cosine_hbm.1, bf16[2,256]{1,0:T(2,128)(2,1)} %albedo_hbm.1, s32[1,256]{1,0:T(1,128)} %bitcast.5, s32[1,256]{1,0:T(1,128)} %bitcast.6, bf16[64,224]{1,0:T(8,128)(2,1)} %gas_hbm.1, ...), custom_call_target="tpu_custom_call" | custom-call | flops 200000000 | bytes 2200000 | tf_op jit(solution)/shard_map/pallas_call | solution.py:339
  33.1 0.6 %copy.13 = f32[64,256]{1,0:T(8,128)} copy(f32[64,256]{1,0:T(8,128)S(1)} %get-tuple-element.2) | data formatting | bytes 131072
  33.8 0.5 %copy.14 = f32[1,64]{1,0:T(1,128)} copy(f32[1,64]{1,0:T(1,128)S(1)} %get-tuple-element.3) | data formatting | bytes 512

commit v8 on v7

--- a/solution.py
+++ b/solution.py
@@ -176,10 +176,10 @@
                     )
                     t_one = tau - 0.98 * ray
                     t_two = tau - slope * ray
-                    product = t_one * t_two
-                    root = lax.rsqrt(product)
-                    x = product * root
-                    sigma = t_one * root
+                    root = lax.rsqrt(t_two)
+                    first_root = t_one * lax.rsqrt(t_one)
+                    x = first_root * (t_two * root)
+                    sigma = first_root * root
                     th = jnp.tanh(x)
                     e = jnp.exp2(x * (-LOG2E))
                     sech = e + e * th

time: 34.4 us -> 34.9 us (1.015)
  Pallas kernels: 32.5 us -> 33 us
    pallas_call x1, Pallas kernels: 32.5 us -> 33 us  [columns_absorbed(): pl.pallas_call(column_kernel, out_shape=(pltpu.VMEM((LEV, 2 * LANES), f32...]
where the time goes in v8:
time: 34.9 us; the launch traced here: 34.8 us
  Pallas kernels  33 us (95%)
  local copies, waits for them, and re-layouts  1.14 us (3%)
  between operations  0.64 us (2%)
    pallas_call x1, Pallas kernels, columns_absorbed(): pl.pallas_call(column_kernel, out_shape=(pltpu.VMEM((LEV, 2 * LANES), f32...  33 us
    unnamed x2, local copies, waits for them, and re-layouts  1.14 us

profile of v8, /device:TPU:1, one launch (start us, length us, event | category | flops | bytes accessed | tf_op | source)
XLA Modules:
  0.0 34.8 jit_solution(17093012728628808030)
XLA Ops:
  0.6 33.0 %shard_map.104 = (f32[64,256]{1,0:T(8,128)S(1)}, f32[1,64]{1,0:T(1,128)S(1)}) custom-call(bf16[256,4096]{1,0:T(8,128)(2,1)} %feat_hbm.1, bf16[256]{0:T(256)(128)(2,1)} %cosine_hbm.1, bf16[2,256]{1,0:T(2,128)(2,1)} %albedo_hbm.1, s32[1,256]{1,0:T(1,128)} %bitcast.5, s32[1,256]{1,0:T(1,128)} %bitcast.6, bf16[64,224]{1,0:T(8,128)(2,1)} %gas_hbm.1, ...), custom_call_target="tpu_custom_call" | custom-call | flops 200000000 | bytes 2200000 | tf_op jit(solution)/shard_map/pallas_call | solution.py:339
  33.6 0.6 %copy.13 = f32[64,256]{1,0:T(8,128)} copy(f32[64,256]{1,0:T(8,128)S(1)} %get-tuple-element.2) | data formatting | bytes 131072
  34.3 0.5 %copy.14 = f32[1,64]{1,0:T(1,128)} copy(f32[1,64]{1,0:T(1,128)S(1)} %get-tuple-element.3) | data formatting | bytes 512

commit v9 on v8

--- a/solution.py
+++ b/solution.py
@@ -38,11 +38,15 @@
 ):
     f32 = jnp.float32
     bf16 = jnp.bfloat16
+    head = 12 * LANES
+    pieces = ((0, 0, head), (0, head, LEV * NF - head), (LANES, 0, LEV * NF))
     chunks = [
         pltpu.make_async_copy(
-            feat_hbm.at[pl.ds(n * LANES, LANES), :], feat_ref.at[pl.ds(n * LANES, LANES), :], feat_sem.at[n]
+            feat_hbm.at[pl.ds(top, LANES), pl.ds(left_edge, width)],
+            feat_ref.at[pl.ds(top, LANES), pl.ds(left_edge, width)],
+            feat_sem.at[n],
         )
-        for n in range(2)
+        for n, (top, left_edge, width) in enumerate(pieces)
     ]
     small = [
         pltpu.make_async_copy(src, dst, small_sem.at[n])
@@ -54,9 +58,9 @@
             )
         )
     ]
+    for copy in small:
+        copy.start()
     for copy in chunks:
-        copy.start()
-    for copy in small:
         copy.start()
 
     n_lon, n_lat = lax.axis_size("lon"), lax.axis_size("lat")
@@ -136,7 +140,7 @@
 
         @pl.when(block == 1)
         def _():
-            chunks[1].wait()
+            chunks[2].wait()
 
         lanes = pl.ds(pl.multiple_of(block * LANES, LANES), LANES)
         cosine = wide_ref[:, lanes]
@@ -212,6 +216,10 @@
         optical(3, depth_3)
 
         def down(step, inner_carry):
+            @pl.when((block == 0) & (step == 1))
+            def _():
+                chunks[1].wait()
+
             @pl.when((block == 0) & (step == PAIRS // 8 - 1))
             def _():
                 pl.semaphore_wait(barrier, chips)
@@ -376,7 +384,7 @@
             pltpu.VMEM((chips, LANES), f32),
             pltpu.VMEM((chips, 1, LANES), f32),
             pltpu.VMEM((chips - 1, 1, LANES), f32),
-            dma((8,)), dma((2,)), dma((chips,)), dma((chips,)), dma((2,)), dma((2,)), dma((chips,)), dma((chips,)),
+            dma((8,)), dma((3,)), dma((chips,)), dma((chips,)), dma((2,)), dma((2,)), dma((chips,)), dma((chips,)),
         ],
         compiler_params=pltpu.CompilerParams(collective_id=0, has_side_effects=True, vmem_limit_bytes=60 * 1024 * 1024),
         cost_estimate=pl.CostEstimate(flops=200_000_000, bytes_accessed=2_200_000, transcendentals=10_000_000),

time: 34.9 us -> 34.6 us (level)
  no operation moved by 1% of the time
where the time goes in v9:
time: 34.6 us; the launch traced here: 34.5 us
  Pallas kernels  32.7 us (95%)
  local copies, waits for them, and re-layouts  1.14 us (3%)
  between operations  0.64 us (2%)
    pallas_call x1, Pallas kernels, columns_absorbed(): pl.pallas_call(column_kernel, out_shape=(pltpu.VMEM((LEV, 2 * LANES), f32...  32.7 us
    unnamed x2, local copies, waits for them, and re-layouts  1.14 us

profile of v9, /device:TPU:1, one launch (start us, length us, event | category | flops | bytes accessed | tf_op | source)
XLA Modules:
  0.0 34.5 jit_solution(9243469508802778364)
XLA Ops:
  0.6 32.7 %shard_map.104 = (f32[64,256]{1,0:T(8,128)S(1)}, f32[1,64]{1,0:T(1,128)S(1)}) custom-call(bf16[256,4096]{1,0:T(8,128)(2,1)} %feat_hbm.1, bf16[256]{0:T(256)(128)(2,1)} %cosine_hbm.1, bf16[2,256]{1,0:T(2,128)(2,1)} %albedo_hbm.1, s32[1,256]{1,0:T(1,128)} %bitcast.5, s32[1,256]{1,0:T(1,128)} %bitcast.6, bf16[64,224]{1,0:T(8,128)(2,1)} %gas_hbm.1, ...), custom_call_target="tpu_custom_call" | custom-call | flops 200000000 | bytes 2200000 | tf_op jit(solution)/shard_map/pallas_call | solution.py:347
  33.3 0.6 %copy.13 = f32[64,256]{1,0:T(8,128)} copy(f32[64,256]{1,0:T(8,128)S(1)} %get-tuple-element.2) | data formatting | bytes 131072
  34.0 0.5 %copy.14 = f32[1,64]{1,0:T(1,128)} copy(f32[1,64]{1,0:T(1,128)S(1)} %get-tuple-element.3) | data formatting | bytes 512
